TPU v7x, 512 devices: a whole 4x4x16 slice. The times are simulated.
512 devices in a mesh: ctx: 64 (over y, z_hi, x, core), tp: 8 (over z_lo).
Axes of the slice: x: 4, y: 4, z: 16 (z_hi: 2, z_lo: 8; z = z_hi * 8 + z_lo), core: 2. Of those that a mesh axis runs over, the one named last changes fastest.
Arguments:
- features: bfloat16 [3, 8192, 4096], P(None, 'ctx', 'tp'), may hold values from -60 to 60
- short_taps: float32 [3, 7, 4096], P(None, None, 'tp'), may hold values from -2.5 to 2.5
- long_filter: bfloat16 [8192, 4096], P('ctx', 'tp'), may hold values from -0.8 to 0.8
- gain: float32 [4096], P('tp'), may hold values from 0.5 to 1.5
- out_grad: bfloat16 [8192, 4096], P('ctx', 'tp'), may hold values from -6 to 6
Outputs:
- normed: bfloat16 [8192, 4096], P('ctx', 'tp')
- feature_grad: bfloat16 [3, 8192, 4096], P(None, 'ctx', 'tp')
- filter_grad: bfloat16 [8192, 4096], P('ctx', 'tp')
- taps_grad: float32 [3, 7, 4096], P(None, None, 'tp')
- gain_grad: float32 [4096], P('tp')
All inputs are finite; a program needn't handle non-finite values.
Results may differ from a plain program's by a relative error of at most 0.0076.
Values may be sent and summed in bfloat16 or wider, within the bound.
A program may use at most 64 MiB of HBM per device.

v0:
```python
import math

import jax
import jax.numpy as jnp
from jax import lax
from jax.sharding import PartitionSpec as P

PRECISE = lax.Precision.HIGHEST
norm_eps = 1e-06


def passed_along(block, axis, distance):
    devices = range(lax.axis_size(axis))
    route = [(i - distance, i) for i in devices if i - distance in devices]
    return lax.ppermute(block, axis, route)


def spin_table(row_count, col_count, period, sign):
    row_ids = lax.broadcasted_iota(jnp.int32, (row_count, col_count), 0)
    col_ids = lax.broadcasted_iota(jnp.int32, (row_count, col_count), 1)
    angles = (row_ids * col_ids % period).astype(jnp.float32) * (2.0 * math.pi / period)
    return (jnp.cos(angles), sign * jnp.sin(angles))


def complex_mix(left_re, left_im, right_re, right_im):
    return (left_re * right_re - left_im * right_im, left_re * right_im + left_im * right_re)


def forward_spectrum(signal):
    stack_size, seq_rows, chan_count = signal.shape
    ctx_size = lax.axis_size("ctx")
    short_side = seq_rows // 2
    long_side = 4 * ctx_size
    half_side = long_side // 2
    full_length = short_side * long_side
    slice_width = short_side // ctx_size
    blocks = signal.reshape(stack_size, 2, short_side, chan_count)
    columns = lax.all_to_all(blocks, "ctx", split_axis=2, concat_axis=1, tiled=True)
    values = columns.astype(jnp.float32)
    cos_one, sin_one = spin_table(half_side, long_side, long_side, -1.0)
    part_re = jnp.einsum("bnic,nk->bkic", values, cos_one, precision=PRECISE)
    part_im = jnp.einsum("bnic,nk->bkic", values, sin_one, precision=PRECISE)
    time_ids = lax.axis_index("ctx") * slice_width + lax.broadcasted_iota(
        jnp.int32, (long_side, slice_width), 1
    )
    freq_ids = lax.broadcasted_iota(jnp.int32, (long_side, slice_width), 0)
    angles = (freq_ids * time_ids % full_length).astype(jnp.float32) * (2.0 * math.pi / full_length)
    turn_re = jnp.cos(angles)[None, :, :, None]
    turn_im = -jnp.sin(angles)[None, :, :, None]
    part_re, part_im = complex_mix(part_re, part_im, turn_re, turn_im)
    part_re, part_im = (
        lax.all_to_all(part_re, "ctx", split_axis=1, concat_axis=2, tiled=True),
        lax.all_to_all(part_im, "ctx", split_axis=1, concat_axis=2, tiled=True),
    )
    cos_two, sin_two = spin_table(short_side, short_side, short_side, -1.0)
    out_re = jnp.einsum("bknc,nj->bkjc", part_re, cos_two, precision=PRECISE) - jnp.einsum(
        "bknc,nj->bkjc", part_im, sin_two, precision=PRECISE
    )
    out_im = jnp.einsum("bknc,nj->bkjc", part_re, sin_two, precision=PRECISE) + jnp.einsum(
        "bknc,nj->bkjc", part_im, cos_two, precision=PRECISE
    )
    return (out_re, out_im)


def inverse_signal(spec_re, spec_im):
    stack_size, local_freq, short_side, chan_count = spec_re.shape
    ctx_size = lax.axis_size("ctx")
    long_side = 4 * ctx_size
    half_side = long_side // 2
    full_length = short_side * long_side
    cos_two, sin_two = spin_table(short_side, short_side, short_side, 1.0)
    mixed_re = jnp.einsum("bkjc,jn->bknc", spec_re, cos_two, precision=PRECISE) - jnp.einsum(
        "bkjc,jn->bknc", spec_im, sin_two, precision=PRECISE
    )
    mixed_im = jnp.einsum("bkjc,jn->bknc", spec_re, sin_two, precision=PRECISE) + jnp.einsum(
        "bkjc,jn->bknc", spec_im, cos_two, precision=PRECISE
    )
    freq_ids = lax.axis_index("ctx") * local_freq + lax.broadcasted_iota(
        jnp.int32, (local_freq, short_side), 0
    )
    time_ids = lax.broadcasted_iota(jnp.int32, (local_freq, short_side), 1)
    angles = (freq_ids * time_ids % full_length).astype(jnp.float32) * (2.0 * math.pi / full_length)
    turn_re = jnp.cos(angles)[None, :, :, None]
    turn_im = jnp.sin(angles)[None, :, :, None]
    mixed_re, mixed_im = complex_mix(mixed_re, mixed_im, turn_re, turn_im)
    mixed_re, mixed_im = (
        lax.all_to_all(mixed_re, "ctx", split_axis=2, concat_axis=1, tiled=True),
        lax.all_to_all(mixed_im, "ctx", split_axis=2, concat_axis=1, tiled=True),
    )
    cos_one, sin_one = spin_table(long_side, half_side, long_side, 1.0)
    restored = jnp.einsum("bkic,kn->bnic", mixed_re, cos_one, precision=PRECISE) - jnp.einsum(
        "bkic,kn->bnic", mixed_im, sin_one, precision=PRECISE
    )
    restored = (restored * (1.0 / full_length)).astype(jnp.bfloat16)
    returned = lax.all_to_all(restored, "ctx", split_axis=1, concat_axis=2, tiled=True)
    return returned.reshape(stack_size, 2 * short_side, chan_count)


def per_device(features, short_taps, long_filter, gain, out_grad):
    tap_count = short_taps.shape[1]
    rim_rows = tap_count - 1
    seq_rows = features.shape[1]
    earlier = passed_along(features[:, seq_rows - rim_rows :, :], "ctx", 1)
    padded = jnp.concatenate([earlier, features], axis=1)
    running = jnp.zeros(features.shape, jnp.float32)
    for lag_id in range(tap_count):
        window = padded[:, rim_rows - lag_id : rim_rows - lag_id + seq_rows, :].astype(jnp.float32)
        running = running + short_taps[:, lag_id, None, :] * window
    shorted = running.astype(jnp.bfloat16)
    q_short = shorted[0].astype(jnp.float32)
    k_short = shorted[1].astype(jnp.float32)
    v_short = shorted[2].astype(jnp.float32)
    product = (k_short * v_short).astype(jnp.bfloat16)
    spec_re, spec_im = forward_spectrum(jnp.stack([long_filter, product]))
    filt_re, filt_im = (spec_re[0], spec_im[0])
    prod_re, prod_im = (spec_re[1], spec_im[1])
    conv_re, conv_im = complex_mix(prod_re, prod_im, filt_re, filt_im)
    convolved = inverse_signal(conv_re[None], conv_im[None])[0]
    conv_full = convolved.astype(jnp.float32)
    gated = q_short * conv_full
    channels = gated.shape[1] * lax.axis_size("tp")
    sum_sq = lax.psum(jnp.sum(gated * gated, axis=1), "tp")
    scale = lax.rsqrt(sum_sq / channels + norm_eps)
    normed = (gated * scale[:, None] * gain[None, :]).astype(jnp.bfloat16)
    upstream = out_grad.astype(jnp.float32)
    weighted = gain[None, :] * upstream
    sum_again, tilt = lax.psum(
        (jnp.sum(gated * gated, axis=1), jnp.sum(weighted * gated, axis=1)), "tp"
    )
    scale_back = lax.rsqrt(sum_again / channels + norm_eps)
    grad_gated = scale_back[:, None] * weighted - gated * (scale_back**3 * tilt / channels)[:, None]
    gain_local = jnp.sum(upstream * gated * scale_back[:, None], axis=0)
    grad_conv = (grad_gated * q_short).astype(jnp.bfloat16)
    back_re, back_im = forward_spectrum(jnp.stack([grad_conv, product]))
    grad_re, grad_im = (back_re[0], back_im[0])
    prod_re, prod_im = (back_re[1], back_im[1])
    lag_f_re, lag_f_im = complex_mix(grad_re, grad_im, filt_re, -filt_im)
    lag_p_re, lag_p_im = complex_mix(grad_re, grad_im, prod_re, -prod_im)
    both = inverse_signal(jnp.stack([lag_f_re, lag_p_re]), jnp.stack([lag_f_im, lag_p_im]))
    grad_product = both[0].astype(jnp.float32)
    filter_grad = both[1]
    grad_short = jnp.stack(
        [grad_gated * conv_full, grad_product * v_short, grad_product * k_short]
    ).astype(jnp.bfloat16)
    later = passed_along(grad_short[:, :rim_rows, :], "ctx", -1)
    tail = jnp.concatenate([grad_short, later], axis=1)
    collected = jnp.zeros(features.shape, jnp.float32)
    for lag_id in range(tap_count):
        collected = collected + short_taps[:, lag_id, None, :] * tail[
            :, lag_id : lag_id + seq_rows, :
        ].astype(jnp.float32)
    feature_grad = collected.astype(jnp.bfloat16)
    grad_short_full = grad_short.astype(jnp.float32)
    taps_local = jnp.stack(
        [
            jnp.sum(
                grad_short_full
                * padded[:, rim_rows - lag_id : rim_rows - lag_id + seq_rows, :].astype(
                    jnp.float32
                ),
                axis=1,
            )
            for lag_id in range(tap_count)
        ],
        axis=1,
    )
    taps_grad, gain_grad = lax.psum((taps_local, gain_local), "ctx")
    return (normed, feature_grad, filter_grad, taps_grad, gain_grad)


def solution(mesh):
    return jax.shard_map(
        per_device,
        mesh=mesh,
        in_specs=(
            P(None, "ctx", "tp"),
            P(None, None, "tp"),
            P("ctx", "tp"),
            P("tp"),
            P("ctx", "tp"),
        ),
        out_specs=(
            P("ctx", "tp"),
            P(None, "ctx", "tp"),
            P("ctx", "tp"),
            P(None, None, "tp"),
            P("tp"),
        ),
        check_vma=False,
    )
```

profile of v0, /device:TPU:1, one launch (start us, length us, event | category | flops | bytes accessed | tf_op | source)
XLA Modules:
  0.0 1155.9 jit_solution(9795879131556582081)
XLA Ops:
  1.4 4.5 collective-permute-start
  15.4 27.0 %all-to-all-start = ((bf16[2,2,64,512]{3,1,0,2:T(2,128)(2,1)}), bf16[2,2,64,512]{3,1,0,2:T(2,128)(2,1)S(1)}, u32[]{:S(2)}, u32[]{:S(2)}) async-start(bf16[2,2,64,512]{3,1,0,2:T(2,128)(2,1)} %copy.59), calls=%async_computation | async-start | bytes 524288 | tf_op jit(solution)/shard_map/all_to_all | solution.py:38
  42.5 18.8 %all-to-all-done = bf16[2,2,64,512]{3,1,0,2:T(2,128)(2,1)S(1)} async-done(((bf16[2,2,64,512]{3,1,0,2:T(2,128)(2,1)}), bf16[2,2,64,512]{3,1,0,2:T(2,128)(2,1)S(1)}, u32[]{:S(2)}, u32[]{:S(2)}) %all-to-all-start) | async-done | bytes 262176 | tf_op jit(solution)/shard_map/all_to_all | solution.py:38
  65.6 4.7 all-to-all-start.1
  72.1 54.2 %all-to-all-done.1 = f32[2,256,1,512]{3,0,2,1:T(2,128)S(1)} async-done(((f32[2,256,1,512]{3,0,2,1:T(2,128)}), f32[2,256,1,512]{3,0,2,1:T(2,128)S(1)}, u32[]{:S(2)}, u32[]{:S(2)}) %all-to-all-start.1) | async-done | bytes 1048608 | tf_op jit(solution)/shard_map/all_to_all | solution.py:52
  135.7 49.9 %all-to-all-done.2 = f32[2,256,1,512]{3,0,2,1:T(2,128)S(1)} async-done(((f32[2,256,1,512]{3,0,2,1:T(2,128)}), f32[2,256,1,512]{3,0,2,1:T(2,128)S(1)}, u32[]{:S(2)}, u32[]{:S(2)}) %all-to-all-start.2) | async-done | bytes 1048608 | tf_op jit(solution)/shard_map/all_to_all | solution.py:53
  194.7 4.7 all-to-all-start.4
  200.5 20.4 %all-to-all-done.4 = f32[1,4,64,512]{3,1,0,2:T(4,128)S(1)} async-done(((f32[1,4,64,512]{3,1,0,2:T(4,128)}), f32[1,4,64,512]{3,1,0,2:T(4,128)S(1)}, u32[]{:S(2)}, u32[]{:S(2)}) %all-to-all-start.4) | async-done | bytes 524320 | tf_op jit(solution)/shard_map/all_to_all | solution.py:88
  220.9 11.1 all-to-all-start.3
  232.2 21.0 %all-to-all-done.3 = f32[1,4,64,512]{3,1,0,2:T(4,128)S(1)} async-done(((f32[1,4,64,512]{3,1,0,2:T(4,128)}), f32[1,4,64,512]{3,1,0,2:T(4,128)S(1)}, u32[]{:S(2)}, u32[]{:S(2)}) %all-to-all-start.3) | async-done | bytes 524320 | tf_op jit(solution)/shard_map/all_to_all | solution.py:87
  257.5 21.7 %all_to_all.186 = bf16[64,2,512]{2,1,0:T(2,128)(2,1)S(1)} all-to-all(bf16[64,2,512]{2,1,0:T(2,128)(2,1)S(1)} %reshape.190), channel_id=1, replica_groups=mesh['ctx'=64,'tp'=8] {'ctx'}, dimensions={0} | all-to-all | bytes 262144 | tf_op jit(solution)/shard_map/all_to_all | solution.py:95
  279.5 25.0 %psum.31 = f32[128]{0:T(128)S(1)} all-reduce(f32[128]{0:T(128)S(1)} %multiply_reduce_fusion), channel_id=1, replica_groups=mesh['ctx'=64,'tp'=8] {'tp'}, use_global_device_ids=true, to_apply=%region_1.2 | all-reduce | flops 128 | bytes 1024 | tf_op jit(solution)/shard_map/psum | solution.py:122
  305.3 21.5 %psum.32 = f32[128]{0:T(128)S(1)} all-reduce(f32[128]{0:T(128)S(1)} %get-tuple-element.27), channel_id=1, replica_groups=mesh['ctx'=64,'tp'=8] {'tp'}, use_global_device_ids=true, to_apply=%region_3.4 | all-reduce | flops 128 | bytes 1024 | tf_op jit(solution)/shard_map/psum | solution.py:127
  328.0 29.9 %all_to_all.187 = bf16[2,2,64,512]{3,1,0,2:T(2,128)(2,1)S(1)} all-to-all(bf16[2,2,64,512]{3,1,0,2:T(2,128)(2,1)S(1)} %copy.69), channel_id=1, replica_groups=mesh['ctx'=64,'tp'=8] {'ctx'}, dimensions={2} | all-to-all | bytes 524288 | tf_op jit(solution)/shard_map/all_to_all | solution.py:38
  363.9 9.9 all-to-all-start.7
  375.6 40.9 %all-to-all-done.7 = f32[2,256,1,512]{3,0,2,1:T(2,128)S(1)} async-done(((f32[2,256,1,512]{3,0,2,1:T(2,128)}), f32[2,256,1,512]{3,0,2,1:T(2,128)S(1)}, u32[]{:S(2)}, u32[]{:S(2)}) %all-to-all-start.7) | async-done | bytes 1048608 | tf_op jit(solution)/shard_map/all_to_all | solution.py:52
  416.5 14.0 %all-to-all-start.8 = ((f32[2,256,1,512]{3,0,2,1:T(2,128)}), f32[2,256,1,512]{3,0,2,1:T(2,128)S(1)}, u32[]{:S(2)}, u32[]{:S(2)}) async-start(f32[2,256,1,512]{3,0,2,1:T(2,128)} %copy.73), calls=%async_computation.8 | async-start | bytes 2097152 | tf_op jit(solution)/shard_map/all_to_all | solution.py:53
  435.7 35.4 %all-to-all-done.8 = f32[2,256,1,512]{3,0,2,1:T(2,128)S(1)} async-done(((f32[2,256,1,512]{3,0,2,1:T(2,128)}), f32[2,256,1,512]{3,0,2,1:T(2,128)S(1)}, u32[]{:S(2)}, u32[]{:S(2)}) %all-to-all-start.8) | async-done | bytes 1048608 | tf_op jit(solution)/shard_map/all_to_all | solution.py:53
  483.0 13.9 %all-to-all-start.10 = ((f32[2,4,64,512]{3,1,0,2:T(4,128)}), f32[2,4,64,512]{3,1,0,2:T(4,128)S(1)}, u32[]{:S(2)}, u32[]{:S(2)}) async-start(f32[2,4,64,512]{3,1,0,2:T(4,128)} %copy.78), calls=%async_computation.10 | async-start | bytes 2097152 | tf_op jit(solution)/shard_map/all_to_all | solution.py:88
  498.6 27.3 %all-to-all-done.10 = f32[2,4,64,512]{3,1,0,2:T(4,128)S(1)} async-done(((f32[2,4,64,512]{3,1,0,2:T(4,128)}), f32[2,4,64,512]{3,1,0,2:T(4,128)S(1)}, u32[]{:S(2)}, u32[]{:S(2)}) %all-to-all-start.10) | async-done | bytes 1048608 | tf_op jit(solution)/shard_map/all_to_all | solution.py:88
  526.0 8.1 all-to-all-start.9
  534.6 40.1 %all-to-all-done.9 = f32[2,4,64,512]{3,1,0,2:T(4,128)S(1)} async-done(((f32[2,4,64,512]{3,1,0,2:T(4,128)}), f32[2,4,64,512]{3,1,0,2:T(4,128)S(1)}, u32[]{:S(2)}, u32[]{:S(2)}) %all-to-all-start.9) | async-done | bytes 1048608 | tf_op jit(solution)/shard_map/all_to_all | solution.py:87
  578.1 28.2 %all_to_all.188 = bf16[2,128,1,512]{3,0,2,1:T(2,128)(2,1)S(1)} all-to-all(bf16[2,128,1,512]{3,0,2,1:T(2,128)(2,1)S(1)} %copy.81), channel_id=1, replica_groups=mesh['ctx'=64,'tp'=8] {'ctx'}, dimensions={1} | all-to-all | bytes 524288 | tf_op jit(solution)/shard_map/all_to_all | solution.py:95
  612.3 540.6 %all-reduce = (f32[3,7,512]{2,0,1:T(4,128)S(1)}, f32[512]{0:T(512)}) all-reduce(f32[3,7,512]{2,0,1:T(4,128)S(1)} %constant_dynamic-update-slice_fusion, f32[512]{0:T(512)S(1)} %copy-done.33), channel_id=1, replica_groups=mesh['ctx'=64,'tp'=8] {'ctx'}, use_global_device_ids=true, to_apply=%region_11.12 | all-reduce | flops 11264 | bytes 90112 | tf_op jit(solution)/shard_map/psum | solution.py:167
  (157 shorter events, 81.5 us)
Async XLA Ops:
  0.6 5.3 copy-start.23
  1.4 8.8 collective-permute-start
  6.0 4.3 copy-start.13
  6.0 4.2 copy-start.15
  6.0 4.2 copy-start.17
  6.0 4.2 copy-start.19
  6.1 7.4 copy-start.21
  10.2 3.2 copy-start.11
  15.4 45.8 %all-to-all-start = ((bf16[2,2,64,512]{3,1,0,2:T(2,128)(2,1)}), bf16[2,2,64,512]{3,1,0,2:T(2,128)(2,1)S(1)}, u32[]{:S(2)}, u32[]{:S(2)}) async-start(bf16[2,2,64,512]{3,1,0,2:T(2,128)(2,1)} %copy.59), calls=%async_computation | async-start | bytes 524288 | tf_op jit(solution)/shard_map/all_to_all | solution.py:38
  42.4 20.1 %copy-start.28 = (f32[256]{0:T(256)}, f32[256]{0:T(256)S(1)}, u32[]{:S(2)}) copy-start(f32[256]{0:T(256)S(1)} %get-tuple-element.71) | copy-start | bytes 3076
  42.5 20.1 %copy-start.30 = (f32[256]{0:T(256)}, f32[256]{0:T(256)S(1)}, u32[]{:S(2)}) copy-start(f32[256]{0:T(256)S(1)} %get-tuple-element.72) | copy-start | bytes 3076
  65.6 60.7 %all-to-all-start.1 = ((f32[2,256,1,512]{3,0,2,1:T(2,128)}), f32[2,256,1,512]{3,0,2,1:T(2,128)S(1)}, u32[]{:S(2)}, u32[]{:S(2)}) async-start(f32[2,256,1,512]{3,0,2,1:T(2,128)} %copy.61), calls=%async_computation.1 | async-start | bytes 2097152 | tf_op jit(solution)/shard_map/all_to_all | solution.py:52
  126.3 59.3 %all-to-all-start.2 = ((f32[2,256,1,512]{3,0,2,1:T(2,128)}), f32[2,256,1,512]{3,0,2,1:T(2,128)S(1)}, u32[]{:S(2)}, u32[]{:S(2)}) async-start(f32[2,256,1,512]{3,0,2,1:T(2,128)} %copy.63), calls=%async_computation.2 | async-start | bytes 2097152 | tf_op jit(solution)/shard_map/all_to_all | solution.py:53
  194.7 26.2 %all-to-all-start.4 = ((f32[1,4,64,512]{3,1,0,2:T(4,128)}), f32[1,4,64,512]{3,1,0,2:T(4,128)S(1)}, u32[]{:S(2)}, u32[]{:S(2)}) async-start(f32[1,4,64,512]{3,1,0,2:T(4,128)} %copy.66), calls=%async_computation.4 | async-start | bytes 1048576 | tf_op jit(solution)/shard_map/all_to_all | solution.py:88
  220.9 32.3 %all-to-all-start.3 = ((f32[1,4,64,512]{3,1,0,2:T(4,128)}), f32[1,4,64,512]{3,1,0,2:T(4,128)S(1)}, u32[]{:S(2)}, u32[]{:S(2)}) async-start(f32[1,4,64,512]{3,1,0,2:T(4,128)} %copy.65), calls=%async_computation.3 | async-start | bytes 1048576 | tf_op jit(solution)/shard_map/all_to_all | solution.py:87
  279.4 25.1 %copy-start.9 = (bf16[128,512]{1,0:T(8,128)(2,1)S(1)}, bf16[128,512]{1,0:T(8,128)(2,1)}, u32[]{:S(2)}) copy-start(bf16[128,512]{1,0:T(8,128)(2,1)} %param.9) | copy-start | bytes 393220
  279.5 25.0 %copy-start.32 = (f32[512]{0:T(512)S(1)}, f32[512]{0:T(512)}, u32[]{:S(2)}) copy-start(f32[512]{0:T(512)} %param.8) | copy-start | bytes 6148
  363.9 52.5 %all-to-all-start.7 = ((f32[2,256,1,512]{3,0,2,1:T(2,128)}), f32[2,256,1,512]{3,0,2,1:T(2,128)S(1)}, u32[]{:S(2)}, u32[]{:S(2)}) async-start(f32[2,256,1,512]{3,0,2,1:T(2,128)} %copy.71), calls=%async_computation.7 | async-start | bytes 2097152 | tf_op jit(solution)/shard_map/all_to_all | solution.py:52
  416.5 54.6 %all-to-all-start.8 = ((f32[2,256,1,512]{3,0,2,1:T(2,128)}), f32[2,256,1,512]{3,0,2,1:T(2,128)S(1)}, u32[]{:S(2)}, u32[]{:S(2)}) async-start(f32[2,256,1,512]{3,0,2,1:T(2,128)} %copy.73), calls=%async_computation.8 | async-start | bytes 2097152 | tf_op jit(solution)/shard_map/all_to_all | solution.py:53
  471.1 3.0 copy-start.2
  483.0 43.0 %all-to-all-start.10 = ((f32[2,4,64,512]{3,1,0,2:T(4,128)}), f32[2,4,64,512]{3,1,0,2:T(4,128)S(1)}, u32[]{:S(2)}, u32[]{:S(2)}) async-start(f32[2,4,64,512]{3,1,0,2:T(4,128)} %copy.78), calls=%async_computation.10 | async-start | bytes 2097152 | tf_op jit(solution)/shard_map/all_to_all | solution.py:88
  526.0 48.8 %all-to-all-start.9 = ((f32[2,4,64,512]{3,1,0,2:T(4,128)}), f32[2,4,64,512]{3,1,0,2:T(4,128)S(1)}, u32[]{:S(2)}, u32[]{:S(2)}) async-start(f32[2,4,64,512]{3,1,0,2:T(4,128)} %copy.75), calls=%async_computation.9 | async-start | bytes 2097152 | tf_op jit(solution)/shard_map/all_to_all | solution.py:87
  609.0 3.3 copy-start.33
  609.8 543.7 %collective-permute-start.1 = (bf16[3,6,512]{2,1,0:T(8,128)(2,1)S(1)}, bf16[3,6,512]{2,1,0:T(8,128)(2,1)S(1)}, u32[]{:S(2)}, u32[]{:S(2)}) collective-permute-start(bf16[3,6,512]{2,1,0:T(8,128)(2,1)S(1)} %slice.173), channel_id=1, source_target_pairs={{8,0},{16,8},{24,16},{32,24},{40,32},{48,40},{56,48},{64,56},{72,6... | collective-permute-start | bytes 55304 | tf_op jit(solution)/shard_map/ppermute | solution.py:15
  (21 other events, 19.9 us)
where the time goes:
time: 1170 us; the launch traced here: 1160 us
  blocking collectives  667 us (57%)
  waiting for transfers between devices  312 us (27%)
  starting transfers between devices  105 us (9%)
  matrix products  35.2 us (3%)
  local copies, waits for them, and re-layouts  25.2 us (2%)
    psum x1, blocking collectives, per_device(): taps_grad, gain_grad = lax.psum((taps_local, gain_local), 'ctx')  541 us
    all_to_all x2, waiting for transfers between devices, forward_spectrum(): lax.all_to_all(part_re, 'ctx', split_axis=1, concat_axis=2, tiled=True)  95.1 us
    all_to_all x2, waiting for transfers between devices, forward_spectrum(): lax.all_to_all(part_im, 'ctx', split_axis=1, concat_axis=2, tiled=True)  85.2 us
    all_to_all x2, waiting for transfers between devices, inverse_signal(): lax.all_to_all(mixed_re, 'ctx', split_axis=2, concat_axis=1, tiled=True)  61.2 us
    all_to_all x2, blocking collectives, inverse_signal(): lax.all_to_all(restored, 'ctx', split_axis=1, concat_axis=2, tiled=True)  49.9 us
    all_to_all x2, waiting for transfers between devices, inverse_signal(): lax.all_to_all(mixed_im, 'ctx', split_axis=2, concat_axis=1, tiled=True)  47.7 us
    all_to_all x1, blocking collectives, forward_spectrum(): lax.all_to_all(blocks, 'ctx', split_axis=2, concat_axis=1, tiled=True)  29.9 us
    all_to_all x1, starting transfers between devices, forward_spectrum(): lax.all_to_all(blocks, 'ctx', split_axis=2, concat_axis=1, tiled=True)  27 us
  transfers between devices with their start and end apart: 11, of which 10 were waited for; matrix products, arithmetic and copies ran while one was open for 2% of the time, Pallas kernels for 0%

commit v1 on v0

v1 whole, which is shorter than its diff:
```python
import functools

import jax
import jax.numpy as jnp
from jax import lax
from jax.experimental import pallas as pl
from jax.experimental.pallas import tpu as pltpu
from jax.sharding import PartitionSpec as P

F32 = jnp.float32
BF16 = jnp.bfloat16
MESH = pl.DeviceIdType.MESH
norm_eps = 1e-06

TAPS = 7
LANES = 128
GROUP = 8
VMEM = pl.BlockSpec(memory_space=pltpu.VMEM)
ANYWHERE = pl.BlockSpec(memory_space=pl.ANY)


def passed_along(block, axis, distance):
    devices = range(lax.axis_size(axis))
    route = [(i - distance, i) for i in devices if i - distance in devices]
    return lax.ppermute(block, axis, route)


def lane_chunks(width):
    return [slice(start, start + LANES) for start in range(0, width, LANES)]


def each_partner(me, visit):
    row, half, col = me // 16, (me // 8) % 2, me % 8

    def crossing(step, carry):
        partner = ((row + step // 8) % 4) * 16 + (1 - half) * 8 + (col + step % 8) % 8
        visit(partner)
        return carry

    def within(step, carry):
        partner = ((row + step // 8) % 4) * 16 + half * 8 + (col + step % 8) % 8
        visit(partner)
        return carry

    lax.fori_loop(0, 32, crossing, 0)
    lax.fori_loop(1, 32, within, 0)


def greet_all(me):
    barrier = pltpu.get_barrier_semaphore()

    def greet(partner):
        pl.semaphore_signal(barrier, inc=1, device_id={"ctx": partner}, device_id_type=MESH)

    each_partner(me, greet)
    pl.semaphore_wait(barrier, 63)


def start_exchange(me, sources, targets, send_sem, recv_sem, backward=False):
    for source, target, sent, came in zip(sources, targets, send_sem, recv_sem):

        def visit(partner, source=source, target=target, sent=sent, came=came):
            pick = 63 - partner if backward else partner
            pltpu.make_async_remote_copy(
                src_ref=source.at[pick],
                dst_ref=target.at[me],
                send_sem=sent,
                recv_sem=came,
                device_id={"ctx": partner},
                device_id_type=MESH,
            ).start()

        each_partner(me, visit)


def await_bytes(ref, sem):
    pltpu.make_async_copy(ref.at[pl.ds(0, 63)], ref.at[pl.ds(0, 63)], sem).wait()


def exchange_kernel(count, backward, *refs):
    sources, targets = refs[:count], refs[count : 2 * count]
    send_sem, recv_sem, local_sem = refs[2 * count :]
    me = lax.axis_index("ctx")
    greet_all(me)
    start_exchange(
        me,
        sources,
        targets,
        [send_sem.at[i] for i in range(count)],
        [recv_sem.at[i] for i in range(count)],
        backward,
    )
    mine = 63 - me if backward else me
    local = [
        pltpu.make_async_copy(s.at[mine], t.at[me], local_sem.at[i])
        for i, (s, t) in enumerate(zip(sources, targets))
    ]
    for copy in local:
        copy.start()
    for copy in local:
        copy.wait()
    for i in range(count):
        await_bytes(sources[i], send_sem.at[i])
        await_bytes(targets[i], recv_sem.at[i])


def exchange(arrays, collective_id, backward=False):
    count = len(arrays)
    return pl.pallas_call(
        functools.partial(exchange_kernel, count, backward),
        out_shape=[jax.ShapeDtypeStruct(a.shape, a.dtype) for a in arrays],
        in_specs=[ANYWHERE] * count,
        out_specs=[ANYWHERE] * count,
        scratch_shapes=[pltpu.SemaphoreType.DMA((count,))] * 3,
        compiler_params=pltpu.CompilerParams(collective_id=collective_id, has_side_effects=True),
    )(*arrays)


def row_sums_kernel(mine_ref, all_ref, send_sem, recv_sem, local_sem):
    me = lax.axis_index("tp")
    barrier = pltpu.get_barrier_semaphore()
    for step in range(1, 8):
        partner = (me + step) % 8
        pl.semaphore_signal(barrier, inc=1, device_id={"tp": partner}, device_id_type=MESH)
    pl.semaphore_wait(barrier, 7)
    for step in range(1, 8):
        partner = (me + step) % 8
        pltpu.make_async_remote_copy(
            src_ref=mine_ref,
            dst_ref=all_ref.at[me],
            send_sem=send_sem,
            recv_sem=recv_sem,
            device_id={"tp": partner},
            device_id_type=MESH,
        ).start()
    own = pltpu.make_async_copy(mine_ref, all_ref.at[me], local_sem)
    own.start()
    own.wait()
    seven = all_ref.at[pl.ds(0, 7)]
    pltpu.make_async_copy(seven, seven, send_sem).wait()
    pltpu.make_async_copy(seven, seven, recv_sem).wait()


def row_sums(mine, collective_id):
    return pl.pallas_call(
        row_sums_kernel,
        out_shape=jax.ShapeDtypeStruct((8,) + mine.shape, F32),
        in_specs=[VMEM],
        out_specs=VMEM,
        scratch_shapes=[pltpu.SemaphoreType.DMA] * 3,
        compiler_params=pltpu.CompilerParams(collective_id=collective_id, has_side_effects=True),
    )(mine)


def ctx_sum_kernel(mine_ref, total_ref, slots, piece, sems):
    me = lax.axis_index("ctx")
    greet_all(me)
    start_exchange(me, [mine_ref], [slots], [sems.at[0]], [sems.at[1]])
    own = pltpu.make_async_copy(mine_ref.at[me], slots.at[me], sems.at[4])
    own.start()
    own.wait()
    await_bytes(mine_ref, sems.at[0])
    await_bytes(slots, sems.at[1])
    piece[...] = jnp.sum(slots[...], axis=0)

    def visit(partner):
        pltpu.make_async_remote_copy(
            src_ref=piece,
            dst_ref=total_ref.at[me],
            send_sem=sems.at[2],
            recv_sem=sems.at[3],
            device_id={"ctx": partner},
            device_id_type=MESH,
        ).start()

    each_partner(me, visit)
    own = pltpu.make_async_copy(piece, total_ref.at[me], sems.at[4])
    own.start()
    own.wait()
    await_bytes(total_ref, sems.at[2])
    await_bytes(total_ref, sems.at[3])


def ctx_sum(mine, collective_id):
    return pl.pallas_call(
        ctx_sum_kernel,
        out_shape=jax.ShapeDtypeStruct(mine.shape, F32),
        in_specs=[VMEM],
        out_specs=VMEM,
        scratch_shapes=[
            pltpu.VMEM(mine.shape, F32),
            pltpu.VMEM(mine.shape[1:], F32),
            pltpu.SemaphoreType.DMA((5,)),
        ],
        compiler_params=pltpu.CompilerParams(collective_id=collective_id, has_side_effects=True),
    )(mine)


def toeplitz_rows(current, other, first, backward):
    rows = lax.broadcasted_iota(jnp.int32, (16, LANES), 0) + first
    lanes = lax.broadcasted_iota(jnp.int32, (16, LANES), 1)
    current = jnp.broadcast_to(current, (16, LANES))
    other = jnp.broadcast_to(other, (16, LANES))
    if backward:
        mixed = jnp.where(lanes >= LANES - 1 - rows, current, other)
        return pltpu.roll(mixed, first + 1, 1, stride=1, stride_axis=0)
    mixed = jnp.where(lanes < LANES - rows, current, other)
    return pltpu.roll(mixed, first, 1, stride=1, stride_axis=0)


def long_kernel(backward, count, window_ref, *refs):
    inputs, outputs = refs[:count], refs[count : 2 * count]
    windows = refs[2 * count]
    padded, flat = refs[2 * count + 1 : 3 * count + 1], refs[3 * count + 1 :]
    blocks = window_ref.shape[0]
    rows = blocks * GROUP
    edge = jnp.zeros((GROUP, LANES), F32)
    windows[pl.ds(0, GROUP), :] = edge
    windows[pl.ds(rows + GROUP, GROUP), :] = edge
    windows[pl.ds(GROUP, rows), :] = window_ref[...].astype(F32).reshape(rows, LANES)
    for source, pad, work in zip(inputs, padded, flat):
        work[...] = source[...].astype(F32).reshape(rows, LANES)
        if backward:
            spots = lax.broadcasted_iota(jnp.int32, (LANES, LANES), 0) + lax.broadcasted_iota(
                jnp.int32, (LANES, LANES), 1
            )
            mirror = jnp.where(spots == LANES - 1, 1.0, 0.0).astype(BF16)
            work[...] = jnp.dot(work[...].astype(BF16), mirror, preferred_element_type=F32)
        for chan in range(GROUP):
            pad[chan, pl.ds(0, blocks), :] = jnp.zeros((blocks, LANES), F32)
            pad[chan, pl.ds(blocks, blocks), :] = work[pl.ds(chan, blocks, stride=GROUP), :]

    def channel(chan, carry):
        def two_lags(pair, total):
            left, right = [], []
            for lag in (2 * pair, 2 * pair + 1):
                base = pl.multiple_of((lag + 1) * GROUP, GROUP) + chan
                current = windows[pl.ds(base, 1), :]
                other = windows[pl.ds(base + (GROUP if backward else -GROUP), 1), :]
                for first in range(0, LANES, 16):
                    right.append(toeplitz_rows(current, other, first, backward).astype(BF16))
                start = lag + 1 if backward else blocks - lag
                left.append(
                    jnp.concatenate([pad[chan, pl.ds(start, blocks), :] for pad in padded], axis=0)
                )
            return total + jnp.dot(
                jnp.concatenate(left, axis=1).astype(BF16),
                jnp.concatenate(right, axis=0),
                preferred_element_type=F32,
            )

        total = lax.fori_loop(
            0, blocks // 2, two_lags, jnp.zeros((count * blocks, LANES), F32), unroll=blocks // 2
        )
        for i, work in enumerate(flat):
            work[pl.ds(chan, blocks, stride=GROUP), :] = total[i * blocks : (i + 1) * blocks]
        return carry

    lax.fori_loop(0, GROUP, channel, 0)
    for output, work in zip(outputs, flat):
        output[...] = work[...].reshape(blocks, GROUP, LANES).astype(BF16)


def long_convolution(window, inputs, backward):
    count = len(inputs)
    blocks = window.shape[0]
    return pl.pallas_call(
        functools.partial(long_kernel, backward, count),
        out_shape=[jax.ShapeDtypeStruct(window.shape, BF16)] * count,
        in_specs=[VMEM] * (count + 1),
        out_specs=[VMEM] * count,
        scratch_shapes=[pltpu.VMEM(((blocks + 2) * GROUP, LANES), F32)]
        + [pltpu.VMEM((GROUP, 2 * blocks, LANES), F32)] * count
        + [pltpu.VMEM((blocks * GROUP, LANES), F32)] * count,
        compiler_params=pltpu.CompilerParams(vmem_limit_bytes=40 << 20),
    )(window, *inputs)


def to_channel_rows(block, index, target):
    target[pl.ds(16 * index, 16)] = block.T.reshape(16, GROUP, LANES).astype(BF16)


def from_channel_rows(source, index):
    return source[pl.ds(16 * index, 16)].astype(F32).reshape(LANES, LANES).T


def pad_before(pad, stream, earlier_ref, features_ref):
    pad[pl.ds(0, 8), :] = earlier_ref[stream].astype(F32)[8:, :]
    pad[pl.ds(8, LANES), :] = features_ref[stream].astype(F32)


def short_kernel(features_ref, earlier_ref, taps_ref, filter_ref, shorted_ref, filt_ref, prod_ref, pad):
    width = features_ref.shape[2]
    for stream in range(3):
        pad_before(pad, stream, earlier_ref, features_ref)
        for lanes in lane_chunks(width):
            for top in (0, 64):
                running = jnp.zeros((64, LANES), F32)
                for lag in range(TAPS):
                    running = running + taps_ref[stream, lag : lag + 1, lanes] * pad[
                        pl.ds(8 - lag + top, 64), lanes
                    ]
                shorted_ref[stream, pl.ds(top, 64), lanes] = running.astype(BF16)
    for index, lanes in enumerate(lane_chunks(width)):
        product = shorted_ref[1, :, lanes].astype(F32) * shorted_ref[2, :, lanes].astype(F32)
        to_channel_rows(product, index, prod_ref)
        to_channel_rows(filter_ref[:, lanes].astype(F32), index, filt_ref)


def gate_kernel(back_ref, shorted_ref, gain_ref, grad_ref, conv_ref, sums_ref):
    width = conv_ref.shape[1]
    squares = jnp.zeros((LANES, LANES), F32)
    tilts = jnp.zeros((LANES, LANES), F32)
    for index, lanes in enumerate(lane_chunks(width)):
        conv = from_channel_rows(back_ref, index)
        conv_ref[:, lanes] = conv.astype(BF16)
        gated = shorted_ref[0, :, lanes].astype(F32) * conv
        squares = squares + gated * gated
        tilts = tilts + gain_ref[:, lanes] * grad_ref[:, lanes].astype(F32) * gated
    sums_ref[...] = jnp.zeros(sums_ref.shape, F32)
    sums_ref[pl.ds(0, 1), :] = jnp.sum(squares.T, axis=0, keepdims=True)
    sums_ref[pl.ds(1, 1), :] = jnp.sum(tilts.T, axis=0, keepdims=True)


def norm_kernel(
    all_ref, conv_ref, shorted_ref, gain_ref, grad_ref, normed_ref, pieces_ref, first_ref, gain_grad_ref
):
    width = conv_ref.shape[1]
    channels = width * all_ref.shape[0]
    sums = jnp.sum(all_ref[...], axis=0)
    scale = lax.rsqrt(sums[0:1] / channels + norm_eps)
    bend = scale**3 * sums[1:2] / channels
    scale = jnp.broadcast_to(scale, (LANES, LANES)).T
    bend = jnp.broadcast_to(bend, (LANES, LANES)).T
    for index, lanes in enumerate(lane_chunks(width)):
        conv = conv_ref[:, lanes].astype(F32)
        q_short = shorted_ref[0, :, lanes].astype(F32)
        gain = gain_ref[:, lanes]
        upstream = grad_ref[:, lanes].astype(F32)
        gated = q_short * conv
        normed_ref[:, lanes] = (gated * scale * gain).astype(BF16)
        grad_gated = scale * (gain * upstream) - gated * bend
        gain_grad_ref[:, lanes] = jnp.sum(upstream * gated * scale, axis=0, keepdims=True)
        first_ref[:, lanes] = (grad_gated * conv).astype(BF16)
        to_channel_rows(grad_gated * q_short, index, pieces_ref)


def stream_kernel(
    grad_prod_ref,
    grad_filt_ref,
    shorted_ref,
    first_ref,
    features_ref,
    earlier_ref,
    gain_grad_ref,
    filter_grad_ref,
    streams_ref,
    sums_ref,
    pad,
):
    width = first_ref.shape[1]
    chunks = lane_chunks(width)
    sums_ref[...] = jnp.zeros(sums_ref.shape, F32)

    def put(row, index, value):
        spot = row * len(chunks) + index
        sums_ref[spot // 2, pl.ds(spot % 2, 1), :] = value

    for index, lanes in enumerate(chunks):
        filter_grad_ref[:, lanes] = from_channel_rows(grad_filt_ref, index).astype(BF16)
        grad_product = from_channel_rows(grad_prod_ref, index)
        streams_ref[0, :, lanes] = first_ref[:, lanes]
        streams_ref[1, :, lanes] = (grad_product * shorted_ref[2, :, lanes].astype(F32)).astype(BF16)
        streams_ref[2, :, lanes] = (grad_product * shorted_ref[1, :, lanes].astype(F32)).astype(BF16)
        put(3 * TAPS, index, gain_grad_ref[:, lanes])
    for stream in range(3):
        pad_before(pad, stream, earlier_ref, features_ref)
        for index, lanes in enumerate(chunks):
            grads = streams_ref[stream, :, lanes].astype(F32)
            for lag in range(TAPS):
                value = jnp.sum(grads * pad[pl.ds(8 - lag, LANES), lanes], axis=0, keepdims=True)
                put(stream * TAPS + lag, index, value)


def gather_kernel(streams_ref, later_ref, taps_ref, out_ref, pad):
    width = streams_ref.shape[2]
    for stream in range(3):
        pad[pl.ds(0, LANES), :] = streams_ref[stream].astype(F32)
        pad[pl.ds(LANES, 8), :] = later_ref[stream].astype(F32)[:8, :]
        for lanes in lane_chunks(width):
            for top in (0, 64):
                total = jnp.zeros((64, LANES), F32)
                for lag in range(TAPS):
                    total = total + taps_ref[stream, lag : lag + 1, lanes] * pad[
                        pl.ds(lag + top, 64), lanes
                    ]
                out_ref[stream, pl.ds(top, 64), lanes] = total.astype(BF16)


def local(kernel, outs, scratch=()):
    return pl.pallas_call(
        kernel,
        out_shape=[jax.ShapeDtypeStruct(shape, kind) for shape, kind in outs],
        out_specs=[VMEM] * len(outs),
        scratch_shapes=list(scratch),
        compiler_params=pltpu.CompilerParams(vmem_limit_bytes=40 << 20),
    )


def per_device(features, short_taps, long_filter, gain, out_grad):
    seq_rows, width = long_filter.shape
    ctx_size = lax.axis_size("ctx")
    pieces = (ctx_size, width // ctx_size, seq_rows)
    plane = (seq_rows, width)
    streams = (3, seq_rows, width)
    pad = pltpu.VMEM((seq_rows + 8, width), F32)
    gain = gain[None, :]
    earlier = passed_along(features[:, seq_rows - 16 :, :], "ctx", 1)
    shorted, filt, prod = local(short_kernel, [(streams, BF16), (pieces, BF16), (pieces, BF16)], [pad])(
        features, earlier, short_taps, long_filter
    )
    filt, prod = exchange([filt, prod], 0)
    (conv,) = long_convolution(filt, [prod], False)
    (conv,) = exchange([conv], 1)
    conv, sums = local(gate_kernel, [(plane, BF16), ((8, seq_rows), F32)])(conv, shorted, gain, out_grad)
    sums = row_sums(sums, 2)
    normed, grad_conv, first, gain_grad = local(
        norm_kernel, [(plane, BF16), (pieces, BF16), (plane, BF16), ((1, width), F32)]
    )(sums, conv, shorted, gain, out_grad)
    (grad_conv,) = exchange([grad_conv], 3)
    grad_prod, grad_filt = long_convolution(grad_conv, [filt, prod], True)
    grad_prod, grad_filt = exchange([grad_prod, grad_filt], 4, True)
    filter_grad, grad_short, sums = local(
        stream_kernel, [(plane, BF16), (streams, BF16), ((ctx_size, 2, LANES), F32)], [pad]
    )(grad_prod, grad_filt, shorted, first, features, earlier, gain_grad)
    later = passed_along(grad_short[:, :16, :], "ctx", -1)
    (feature_grad,) = local(gather_kernel, [(streams, BF16)], [pad])(grad_short, later, short_taps)
    sums = ctx_sum(sums, 5).reshape(-1)[: (3 * TAPS + 1) * width].reshape(3 * TAPS + 1, width)
    taps_grad = sums[: 3 * TAPS].reshape(3, TAPS, width)
    return (normed, feature_grad, filter_grad, taps_grad, sums[3 * TAPS])


def solution(mesh):
    return jax.shard_map(
        per_device,
        mesh=mesh,
        in_specs=(
            P(None, "ctx", "tp"),
            P(None, None, "tp"),
            P("ctx", "tp"),
            P("tp"),
            P("ctx", "tp"),
        ),
        out_specs=(
            P("ctx", "tp"),
            P(None, "ctx", "tp"),
            P("ctx", "tp"),
            P(None, None, "tp"),
            P("tp"),
        ),
        check_vma=False,
    )
```

time: 1170 us -> 204 us (0.17)
  the two profiles are of different devices: /device:TPU:1 before, /device:TPU:225 now
where the time goes in v1:
time: 204 us; the launch traced here: 203 us
  Pallas kernels  178 us (87%)
  local copies, waits for them, and re-layouts  17.4 us (9%)
  starting transfers between devices  5.96 us (3%)
    pallas_call x4, Pallas kernels, exchange(): pl.pallas_call(functools.partial(exchange_kernel, count, backward), out_s...  113 us
    pallas_call x1, Pallas kernels, ctx_sum(): pl.pallas_call(ctx_sum_kernel, out_shape=jax.ShapeDtypeStruct(mine.shape,...  34.9 us
    unnamed x46, local copies, waits for them, and re-layouts  13.9 us
    pallas_call x2, Pallas kernels, long_convolution(): pl.pallas_call(functools.partial(long_kernel, backward, count), out_shape...  13.8 us
    pallas_call x1, Pallas kernels, row_sums(): pl.pallas_call(row_sums_kernel, out_shape=jax.ShapeDtypeStruct((8,) + min...  11.4 us
    ppermute x2, starting transfers between devices, passed_along(): return lax.ppermute(block, axis, route)  5.96 us
  transfers between devices with their start and end apart: 2, of which 1 were waited for; matrix products, arithmetic and copies ran while one was open for 1% of the time, Pallas kernels for 17%

profile of v1, /device:TPU:225, one launch (start us, length us, event | category | flops | bytes accessed | tf_op | source)
XLA Modules:
  0.0 203.3 jit_solution(5148032540978093037)
XLA Ops:
  1.5 3.7 %collective-permute-start = (bf16[3,16,512]{2,1,0:T(8,128)(2,1)S(1)}, bf16[3,16,512]{2,1,0:T(8,128)(2,1)S(1)}, u32[]{:S(2)}, u32[]{:S(2)}) collective-permute-start(bf16[3,16,512]{2,1,0:T(8,128)(2,1)S(1)} %slice.18), channel_id=1, source_target_pairs={{0,8},{8,16},{16,24},{24,32},{32,40},{40,48},{48,56},{56,64},{64,7... | collective-permute-start | bytes 147464 | tf_op jit(solution)/shard_map/ppermute | solution.py:25
  5.1 1.2 collective-permute-done.earlier_ref
  6.3 1.0 copy-done
  7.3 0.9 copy-done.11
  8.2 1.2 shard_map.92
  10.7 42.1 %shard_map.93 = (bf16[64,8,128]{2,1,0:T(8,128)(2,1)}, bf16[64,8,128]{2,1,0:T(8,128)(2,1)}) custom-call(bf16[64,8,128]{2,1,0:T(8,128)(2,1)} %copy-done.17, bf16[64,8,128]{2,1,0:T(8,128)(2,1)} %copy-done.18), custom_call_target="tpu_custom_call" | custom-call | tf_op jit(solution)/shard_map/pallas_call | solution.py:109
  52.8 0.9 copy-done.2
  53.7 0.9 copy-done.4
  54.6 6.4 %shard_map.94.refs_0_ = bf16[64,8,128]{2,1,0:T(8,128)(2,1)S(1)} custom-call(bf16[64,8,128]{2,1,0:T(8,128)(2,1)S(1)} %copy-done.2, bf16[64,8,128]{2,1,0:T(8,128)(2,1)S(1)} %copy-done.4), custom_call_target="tpu_custom_call" | custom-call | tf_op jit(solution)/shard_map/pallas_call | solution.py:267
  61.7 20.2 %shard_map.95.back_ref = bf16[64,8,128]{2,1,0:T(8,128)(2,1)} custom-call(bf16[64,8,128]{2,1,0:T(8,128)(2,1)} %copy-done.8), custom_call_target="tpu_custom_call" | custom-call | tf_op jit(solution)/shard_map/pallas_call | solution.py:109
  82.6 0.9 copy-done.7
  84.3 11.4 %shard_map.97.all_ref = f32[8,8,128]{2,1,0:T(8,128)} custom-call(f32[8,128]{1,0:T(8,128)} %copy-done.22), custom_call_target="tpu_custom_call" | custom-call | tf_op jit(solution)/shard_map/pallas_call | solution.py:145
  96.5 0.9 shard_map.98
  98.0 23.3 %shard_map.99.window_ref = bf16[64,8,128]{2,1,0:T(8,128)(2,1)} custom-call(bf16[64,8,128]{2,1,0:T(8,128)(2,1)} %copy-done.16), custom_call_target="tpu_custom_call" | custom-call | tf_op jit(solution)/shard_map/pallas_call | solution.py:109
  121.4 0.9 copy-done.6
  122.3 7.4 %shard_map.100 = (bf16[64,8,128]{2,1,0:T(8,128)(2,1)S(1)}, bf16[64,8,128]{2,1,0:T(8,128)(2,1)S(1)}) custom-call(bf16[64,8,128]{2,1,0:T(8,128)(2,1)S(1)} %copy-done.6, bf16[64,8,128]{2,1,0:T(8,128)(2,1)S(1)} %copy-done.3, bf16[64,8,128]{2,1,0:T(8,128)(2,1)S(1)} %copy-done.5), custom_call_target="tpu_custom_call" | custom-call | tf_op jit(solution)/shard_map/pallas_call | solution.py:267
  131.0 27.2 %shard_map.101 = (bf16[64,8,128]{2,1,0:T(8,128)(2,1)}, bf16[64,8,128]{2,1,0:T(8,128)(2,1)}) custom-call(bf16[64,8,128]{2,1,0:T(8,128)(2,1)} %copy-done.14, bf16[64,8,128]{2,1,0:T(8,128)(2,1)} %copy-done.15), custom_call_target="tpu_custom_call" | custom-call | tf_op jit(solution)/shard_map/pallas_call | solution.py:109
  158.2 0.9 copy-done.12
  159.1 0.9 copy-done.13
  160.0 1.3 shard_map.102
  162.0 2.3 %collective-permute-start.1 = (bf16[3,16,512]{2,1,0:T(8,128)(2,1)S(1)}, bf16[3,16,512]{2,1,0:T(8,128)(2,1)S(1)}, u32[]{:S(2)}, u32[]{:S(2)}) collective-permute-start(bf16[3,16,512]{2,1,0:T(8,128)(2,1)S(1)} %slice.19), channel_id=1, source_target_pairs={{8,0},{16,8},{24,16},{32,24},{40,32},{48,40},{56,48},{64,56},{72,6... | collective-permute-start | bytes 147464 | tf_op jit(solution)/shard_map/ppermute | solution.py:25
  164.3 34.9 %shard_map.104 = f32[64,2,128]{2,1,0:T(2,128)} custom-call(f32[64,2,128]{2,1,0:T(2,128)} %copy-done.20), custom_call_target="tpu_custom_call" | custom-call | tf_op jit(solution)/shard_map/pallas_call | solution.py:185
  199.2 1.3 slice.21
  201.9 1.5 shard_map.103
  (45 shorter events, 9.0 us)
Async XLA Ops:
  0.6 5.7 %copy-start.10 = (f32[3,7,512]{2,1,0:T(8,128)S(1)}, f32[3,7,512]{2,1,0:T(8,128)}, u32[]{:S(2)}) copy-start(f32[3,7,512]{2,1,0:T(8,128)} %taps_ref.3) | copy-start | bytes 129028
  1.5 4.8 %collective-permute-start = (bf16[3,16,512]{2,1,0:T(8,128)(2,1)S(1)}, bf16[3,16,512]{2,1,0:T(8,128)(2,1)S(1)}, u32[]{:S(2)}, u32[]{:S(2)}) collective-permute-start(bf16[3,16,512]{2,1,0:T(8,128)(2,1)S(1)} %slice.18), channel_id=1, source_target_pairs={{0,8},{8,16},{16,24},{24,32},{32,40},{40,48},{48,56},{56,64},{64,7... | collective-permute-start | bytes 147464 | tf_op jit(solution)/shard_map/ppermute | solution.py:25
  6.3 1.0 copy-start
  7.3 0.9 copy-start.11
  9.4 0.7 copy-start.17
  10.1 0.7 copy-start.18
  52.8 0.9 copy-start.2
  53.7 0.9 copy-start.4
  61.1 0.7 copy-start.8
  61.7 20.2 %copy-start.9 = (bf16[128,512]{1,0:T(8,128)(2,1)S(1)}, bf16[128,512]{1,0:T(8,128)(2,1)}, u32[]{:S(2)}) copy-start(bf16[128,512]{1,0:T(8,128)(2,1)} %grad_ref.3) | copy-start | bytes 393220
  81.9 0.7 copy-start.21
  82.6 0.9 copy-start.7
  95.7 0.8 copy-start.19
  97.4 0.7 copy-start.16
  98.0 23.3 %copy-start.3 = (bf16[64,8,128]{2,1,0:T(8,128)(2,1)S(1)}, bf16[64,8,128]{2,1,0:T(8,128)(2,1)}, u32[]{:S(2)}) copy-start(bf16[64,8,128]{2,1,0:T(8,128)(2,1)} %get-tuple-element.25.window_ref.refs_0_) | copy-start | bytes 393220
  98.0 23.3 %copy-start.5 = (bf16[64,8,128]{2,1,0:T(8,128)(2,1)S(1)}, bf16[64,8,128]{2,1,0:T(8,128)(2,1)}, u32[]{:S(2)}) copy-start(bf16[64,8,128]{2,1,0:T(8,128)(2,1)} %get-tuple-element.26.refs_0_.refs_1_) | copy-start | bytes 393220
  121.4 0.9 copy-start.6
  122.3 35.9 %copy-start.1 = (bf16[3,128,512]{2,1,0:T(8,128)(2,1)S(1)}, bf16[3,128,512]{2,1,0:T(8,128)(2,1)}, u32[]{:S(2)}) copy-start(bf16[3,128,512]{2,1,0:T(8,128)(2,1)} %features_ref.3) | copy-start | bytes 1179652
  129.7 0.7 copy-start.14
  130.4 0.7 copy-start.15
  158.2 0.9 copy-start.12
  159.1 0.9 copy-start.13
  162.0 39.9 %collective-permute-start.1 = (bf16[3,16,512]{2,1,0:T(8,128)(2,1)S(1)}, bf16[3,16,512]{2,1,0:T(8,128)(2,1)S(1)}, u32[]{:S(2)}, u32[]{:S(2)}) collective-permute-start(bf16[3,16,512]{2,1,0:T(8,128)(2,1)S(1)} %slice.19), channel_id=1, source_target_pairs={{8,0},{16,8},{24,16},{32,24},{40,32},{48,40},{56,48},{64,56},{72,6... | collective-permute-start | bytes 147464 | tf_op jit(solution)/shard_map/ppermute | solution.py:25
  200.4 0.8 slice-start
  (2 other events, 1.2 us)

commit v2 on v0

v2 whole, which is shorter than its diff:
```python
import functools

import jax
import jax.numpy as jnp
from jax import lax
from jax.experimental import pallas as pl
from jax.experimental.pallas import tpu as pltpu
from jax.sharding import PartitionSpec as P

F32 = jnp.float32
BF16 = jnp.bfloat16
MESH = pl.DeviceIdType.MESH
norm_eps = 1e-06

TAPS = 7
LANES = 128
GROUP = 8
VMEM = pl.BlockSpec(memory_space=pltpu.VMEM)


def lane_chunks(width):
    return [slice(start, start + LANES) for start in range(0, width, LANES)]


def each_partner(me, visit, crossing=True, within=True):
    row, half, col = me // 16, (me // 8) % 2, me % 8

    def other_half(step, carry):
        visit(((row + step // 8) % 4) * 16 + (1 - half) * 8 + (col + step % 8) % 8)
        return carry

    def same_half(step, carry):
        visit(((row + step // 8) % 4) * 16 + half * 8 + (col + step % 8) % 8)
        return carry

    if crossing:
        lax.fori_loop(0, 32, other_half, 0)
    if within:
        lax.fori_loop(1, 32, same_half, 0)


def remote(source, target, sems, device):
    return pltpu.make_async_remote_copy(
        src_ref=source,
        dst_ref=target,
        send_sem=sems.at[0],
        recv_sem=sems.at[1],
        device_id=device,
        device_id_type=MESH,
    )


def start_exchange(me, source, target, sems):
    def visit(partner):
        remote(source.at[partner], target.at[me], sems, {"ctx": partner}).start()

    each_partner(me, visit)
    target[pl.ds(me, 1)] = source[pl.ds(me, 1)]


def start_gather(me, piece, target, sems):
    def visit(partner):
        remote(piece, target.at[me], sems, {"ctx": partner}).start()

    each_partner(me, visit)
    target[pl.ds(me, 1)] = piece[...][None]


def await_slots(ref, count, sem):
    slots = ref.at[pl.ds(0, count)]
    pltpu.make_async_copy(slots, slots, sem).wait()


def toeplitz_rows(current, other, first, backward):
    rows = lax.broadcasted_iota(jnp.int32, (16, LANES), 0) + first
    lanes = lax.broadcasted_iota(jnp.int32, (16, LANES), 1)
    current = jnp.broadcast_to(current, (16, LANES))
    other = jnp.broadcast_to(other, (16, LANES))
    if backward:
        mixed = jnp.where(lanes >= LANES - 1 - rows, current, other)
        return pltpu.roll(mixed, first + 1, 1, stride=1, stride_axis=0)
    mixed = jnp.where(lanes < LANES - rows, current, other)
    return pltpu.roll(mixed, first, 1, stride=1, stride_axis=0)


def fill_padded(pad, work, mirrored):
    blocks = pad.shape[1] // 2
    if mirrored:
        spots = lax.broadcasted_iota(jnp.int32, (LANES, LANES), 0) + lax.broadcasted_iota(
            jnp.int32, (LANES, LANES), 1
        )
        mirror = jnp.where(spots == LANES - 1, 1.0, 0.0).astype(BF16)
    for chan in range(GROUP):
        rows = work[pl.ds(chan, blocks, stride=GROUP), :]
        if mirrored:
            rows = jnp.dot(rows.astype(BF16), mirror, preferred_element_type=F32)
        pad[chan, pl.ds(0, blocks), :] = jnp.zeros((blocks, LANES), F32)
        pad[chan, pl.ds(blocks, blocks), :] = rows


def fill_windows(windows, pieces):
    blocks = pieces.shape[0]
    rows = blocks * GROUP
    edge = jnp.zeros((GROUP, LANES), F32)
    windows[pl.ds(0, GROUP), :] = edge
    windows[pl.ds(rows + GROUP, GROUP), :] = edge
    windows[pl.ds(GROUP, rows), :] = pieces[...].astype(F32).reshape(rows, LANES)


def long_products(backward, windows, padded, flat):
    count = len(padded)
    blocks = padded[0].shape[1] // 2

    def channel(chan, carry):
        def two_lags(pair, total):
            left, right = [], []
            for lag in (2 * pair, 2 * pair + 1):
                base = pl.multiple_of((lag + 1) * GROUP, GROUP) + chan
                current = windows[pl.ds(base, 1), :]
                other = windows[pl.ds(base + (GROUP if backward else -GROUP), 1), :]
                for first in range(0, LANES, 16):
                    right.append(toeplitz_rows(current, other, first, backward).astype(BF16))
                start = lag + 1 if backward else blocks - lag
                left.append(
                    jnp.concatenate([pad[chan, pl.ds(start, blocks), :] for pad in padded], axis=0)
                )
            return total + jnp.dot(
                jnp.concatenate(left, axis=1).astype(BF16),
                jnp.concatenate(right, axis=0),
                preferred_element_type=F32,
            )

        total = lax.fori_loop(
            0, blocks // 2, two_lags, jnp.zeros((count * blocks, LANES), F32), unroll=blocks // 2
        )
        for i, work in enumerate(flat):
            work[pl.ds(chan, blocks, stride=GROUP), :] = total[i * blocks : (i + 1) * blocks]
        return carry

    lax.fori_loop(0, GROUP, channel, 0)


def to_pieces(block):
    return block.T.reshape(16, GROUP, LANES).astype(BF16)


def from_pieces(pieces):
    return pieces.astype(F32).reshape(LANES, LANES).T


def owner_taps(taps, stream):
    return [
        jnp.broadcast_to(taps[:, stream * TAPS + lag : stream * TAPS + lag + 1], (GROUP, LANES))
        for lag in range(TAPS)
    ]


def owner_short(raw, which, taps, target):
    lanes = lax.broadcasted_iota(jnp.int32, (GROUP, LANES), 1)

    def block(index, before):
        now = raw[index, which].astype(F32)
        total = taps[0] * now
        after = []
        for lag in range(1, TAPS):
            turned = pltpu.roll(now, lag, 1)
            total = total + taps[lag] * jnp.where(lanes >= lag, turned, before[lag - 1])
            after.append(turned)
        target[pl.ds(pl.multiple_of(index * GROUP, GROUP), GROUP), :] = total.astype(BF16).astype(F32)
        return tuple(after)

    zero = jnp.zeros((GROUP, LANES), F32)
    lax.fori_loop(0, raw.shape[0], block, (zero,) * (TAPS - 1), unroll=8)


def owner_back(raw, which, taps, grad_flat, partner_flat, target, slot):
    lanes = lax.broadcasted_iota(jnp.int32, (GROUP, LANES), 1)
    blocks = raw.shape[0]

    def block(step, carry):
        after, sums = carry
        index = blocks - 1 - step
        grad = grad_flat[pl.ds(pl.multiple_of(step * GROUP, GROUP), GROUP), :].astype(BF16).astype(F32)
        rows = pl.ds(pl.multiple_of(index * GROUP, GROUP), GROUP)
        grad = (grad * partner_flat[rows, :]).astype(BF16).astype(F32)
        value = raw[index, which].astype(F32)
        total = taps[0] * grad
        new_sums = [sums[0] + value * grad]
        new_after = []
        for lag in range(1, TAPS):
            turned = pltpu.roll(grad, LANES - lag, 1)
            moved = jnp.where(lanes < LANES - lag, turned, after[lag - 1])
            total = total + taps[lag] * moved
            new_sums.append(sums[lag] + value * moved)
            new_after.append(turned)
        target[index, slot] = total.astype(BF16)
        return tuple(new_after), tuple(new_sums)

    zero = jnp.zeros((GROUP, LANES), F32)
    _, sums = lax.fori_loop(
        0, blocks, block, ((zero,) * (TAPS - 1), (zero,) * TAPS), unroll=8
    )
    return sums


def block_kernel(
    features_ref,
    taps_ref,
    filter_ref,
    gain_ref,
    grad_ref,
    normed_ref,
    feature_grad_ref,
    filter_grad_ref,
    first_sums_ref,
    owner_sums_ref,
    filt_send,
    filt_recv,
    pair_send,
    pair_recv,
    conv_send,
    conv_recv,
    back_send,
    back_recv,
    out_send,
    out_recv,
    before_recv,
    after_send,
    after_recv,
    row_send,
    row_recv,
    part_send,
    part_recv,
    part_sum,
    first_all,
    owner_sum,
    owner_all,
    taps_turned,
    pad,
    q_short,
    conv,
    windows,
    k_short,
    v_short,
    flat_a,
    flat_b,
    pad_fwd,
    pad_filt,
    pad_prod,
    sems,
):
    me = lax.axis_index("ctx")
    rank = lax.axis_index("tp")
    half = (me // 8) % 2
    width = filter_ref.shape[1]
    chunks = list(enumerate(lane_chunks(width)))
    blocks = filt_recv.shape[0]
    rows = blocks * GROUP
    channels = width * 8
    following = {"ctx": (me + 1) % 64}
    preceding = {"ctx": (me + 63) % 64}

    barrier = pltpu.get_barrier_semaphore()

    def greet(partner):
        pl.semaphore_signal(barrier, inc=1, device_id={"ctx": partner}, device_id_type=MESH)

    each_partner(me, greet)
    for step in range(1, 8):
        pl.semaphore_signal(
            barrier, inc=1, device_id={"tp": (rank + step) % 8}, device_id_type=MESH
        )

    for index, lanes in chunks:
        spot = pl.ds(16 * index, 16)
        filt_send[spot] = to_pieces(filter_ref[:, lanes].astype(F32))
        pair_send[spot, 0] = to_pieces(features_ref[1, :, lanes].astype(F32))
        pair_send[spot, 1] = to_pieces(features_ref[2, :, lanes].astype(F32))
    pl.semaphore_wait(barrier, 70)
    start_exchange(me, filt_send, filt_recv, sems.at[0])
    start_exchange(me, pair_send, pair_recv, sems.at[1])
    last = features_ref.at[0, pl.ds(LANES - 16, 16)]
    remote(last, before_recv, sems.at[2], following).start()

    filler = jnp.zeros((LANES - 3 * TAPS, LANES), F32)
    for index, lanes in chunks:
        stack = jnp.concatenate([taps_ref[i, :, lanes] for i in range(3)] + [filler], axis=0)
        taps_turned[pl.ds(LANES * index, LANES), :] = stack.T
    own_taps = taps_turned[pl.ds(pl.multiple_of(me * GROUP, GROUP), GROUP), :]
    remote(last, before_recv, sems.at[2], following).wait_recv()
    pad[pl.ds(0, 8), :] = jnp.where(me > 0, before_recv[...].astype(F32)[8:, :], 0.0)
    pad[pl.ds(8, LANES), :] = features_ref[0].astype(F32)
    for _, lanes in chunks:
        for top in (0, 64):
            running = jnp.zeros((64, LANES), F32)
            for lag in range(TAPS):
                running = running + taps_ref[0, lag : lag + 1, lanes] * pad[
                    pl.ds(8 - lag + top, 64), lanes
                ]
            q_short[pl.ds(top, 64), lanes] = running.astype(BF16).astype(F32)

    await_slots(filt_recv, 63, sems.at[0, 1])
    fill_windows(windows, filt_recv)
    flat_a[...] = filt_recv[...].astype(F32).reshape(rows, LANES)
    fill_padded(pad_filt, flat_a, True)
    await_slots(pair_recv, 63, sems.at[1, 1])
    k_taps, v_taps = owner_taps(own_taps, 1), owner_taps(own_taps, 2)
    owner_short(pair_recv, 0, k_taps, k_short)
    owner_short(pair_recv, 1, v_taps, v_short)
    flat_b[...] = (k_short[...] * v_short[...]).astype(BF16).astype(F32)
    fill_padded(pad_fwd, flat_b, False)
    long_products(False, windows, [pad_fwd], [flat_a])
    conv_send[...] = flat_a[...].reshape(blocks, GROUP, LANES).astype(BF16)
    start_exchange(me, conv_send, conv_recv, sems.at[3])
    fill_padded(pad_prod, flat_b, True)
    await_slots(conv_recv, 63, sems.at[3, 1])

    squares = jnp.zeros((LANES, LANES), F32)
    tilts = jnp.zeros((LANES, LANES), F32)
    for index, lanes in chunks:
        value = from_pieces(conv_recv[pl.ds(16 * index, 16)])
        conv[:, lanes] = value
        gated = q_short[:, lanes] * value
        squares = squares + gated * gated
        tilts = tilts + gain_ref[:, lanes] * grad_ref[:, lanes].astype(F32) * gated
    row_send[...] = jnp.zeros(row_send.shape, F32)
    row_send[pl.ds(0, 1), :] = jnp.sum(squares.T, axis=0, keepdims=True)
    row_send[pl.ds(1, 1), :] = jnp.sum(tilts.T, axis=0, keepdims=True)
    for step in range(1, 8):
        remote(row_send, row_recv.at[rank], sems.at[4], {"tp": (rank + step) % 8}).start()
    row_recv[pl.ds(rank, 1)] = row_send[...][None]
    await_slots(row_recv, 7, sems.at[4, 1])
    sums = jnp.sum(row_recv[...], axis=0)
    scale = lax.rsqrt(sums[0:1] / channels + norm_eps)
    bend = scale**3 * sums[1:2] / channels
    scale = jnp.broadcast_to(scale, (LANES, LANES)).T
    bend = jnp.broadcast_to(bend, (LANES, LANES)).T

    def gate(lanes):
        value, q_value = conv[:, lanes], q_short[:, lanes]
        gain = gain_ref[:, lanes]
        upstream = grad_ref[:, lanes].astype(F32)
        gated = q_value * value
        grad_gated = scale * (gain * upstream) - gated * bend
        return value, q_value, gain, upstream, gated, grad_gated

    for index, lanes in chunks:
        _, q_value, _, _, _, grad_gated = gate(lanes)
        back_send[pl.ds(16 * index, 16)] = to_pieces(grad_gated * q_value)
    start_exchange(me, back_send, back_recv, sems.at[5])

    for index, lanes in chunks:
        value, _, gain, upstream, gated, grad_gated = gate(lanes)
        normed_ref[:, lanes] = (gated * scale * gain).astype(BF16)
        part_send[7 * 4 + index] = jnp.sum(upstream * gated * scale, axis=0, keepdims=True)
        first = (grad_gated * value).astype(BF16)
        after_send[:, lanes] = first[:16]
        first = first.astype(F32)
        conv[:, lanes] = first
        for lag in range(TAPS):
            part_send[lag * 4 + index] = jnp.sum(
                first * pad[pl.ds(8 - lag, LANES), lanes], axis=0, keepdims=True
            )
    remote(after_send, after_recv, sems.at[6], preceding).start()
    mine = (me // 16) * 8 + me % 8

    def send_part(partner):
        place = (partner // 16) * 8 + partner % 8
        remote(part_send.at[place], part_recv.at[mine], sems.at[7], {"ctx": partner}).start()

    each_partner(me, send_part, crossing=False)
    part_recv[pl.ds(mine, 1)] = part_send[pl.ds(mine, 1)]
    await_slots(part_recv, 31, sems.at[7, 1])
    part_sum[...] = jnp.sum(part_recv[...], axis=0)
    start_gather(me, part_sum, first_all, sems.at[8])

    await_slots(back_recv, 63, sems.at[5, 1])
    fill_windows(windows, back_recv)
    long_products(True, windows, [pad_filt, pad_prod], [flat_a, flat_b])

    def place_filter(index, carry):
        step = pl.multiple_of((blocks - 1 - index) * GROUP, GROUP)
        out_send[index, 0] = flat_b[pl.ds(step, GROUP), :].astype(BF16)
        return carry

    lax.fori_loop(0, blocks, place_filter, 0, unroll=8)
    k_sums = owner_back(pair_recv, 0, k_taps, flat_a, v_short, out_send, 1)
    v_sums = owner_back(pair_recv, 1, v_taps, flat_a, k_short, out_send, 2)
    start_exchange(me, out_send, out_recv, sems.at[9])
    lane_ids = lax.broadcasted_iota(jnp.int32, (GROUP, LANES), 1)
    chan_ids = lax.broadcasted_iota(jnp.int32, (GROUP, LANES), 0)
    packed = jnp.zeros((GROUP, LANES), F32)
    for place, value in enumerate(k_sums + v_sums):
        total = jnp.sum(value, axis=1, keepdims=True)
        packed = packed + jnp.where(lane_ids == place * GROUP + chan_ids, total, 0.0)
    owner_sum[...] = jnp.sum(packed, axis=0, keepdims=True)
    start_gather(me, owner_sum, owner_all, sems.at[10])

    remote(after_send, after_recv, sems.at[6], preceding).wait_recv()
    pad[pl.ds(0, LANES), :] = conv[...]
    pad[pl.ds(LANES, 8), :] = jnp.where(me < 63, after_recv[...].astype(F32)[:8, :], 0.0)
    for _, lanes in chunks:
        for top in (0, 64):
            total = jnp.zeros((64, LANES), F32)
            for lag in range(TAPS):
                total = total + taps_ref[0, lag : lag + 1, lanes] * pad[pl.ds(lag + top, 64), lanes]
            feature_grad_ref[0, pl.ds(top, 64), lanes] = total.astype(BF16)

    await_slots(first_all, 63, sems.at[8, 1])
    first_sums_ref[...] = first_all[...]
    await_slots(out_recv, 63, sems.at[9, 1])
    for index, lanes in chunks:
        spot = pl.ds(16 * index, 16)
        filter_grad_ref[:, lanes] = from_pieces(out_recv[spot, 0]).astype(BF16)
        feature_grad_ref[1, :, lanes] = from_pieces(out_recv[spot, 1]).astype(BF16)
        feature_grad_ref[2, :, lanes] = from_pieces(out_recv[spot, 2]).astype(BF16)
    await_slots(owner_all, 63, sems.at[10, 1])
    owner_sums_ref[...] = owner_all[...]

    for ref, count, number in (
        (filt_recv, 63, 0),
        (pair_recv, 63, 1),
        (conv_recv, 63, 3),
        (row_recv, 7, 4),
        (back_recv, 63, 5),
        (part_recv, 31, 7),
        (first_all, 63, 8),
        (out_recv, 63, 9),
        (owner_all, 63, 10),
    ):
        await_slots(ref, count, sems.at[number, 0])
    remote(last, before_recv, sems.at[2], following).wait_send()
    remote(after_send, after_recv, sems.at[6], preceding).wait_send()


def per_device(features, short_taps, long_filter, gain, out_grad):
    seq_rows, width = long_filter.shape
    blocks = lax.axis_size("ctx")
    pieces = (blocks, GROUP, LANES)
    flat = (blocks * GROUP, LANES)
    padded = (GROUP, 2 * blocks, LANES)
    row = (1, LANES)
    exchanged = [pltpu.VMEM(pieces, BF16)] * 2
    pairs = [pltpu.VMEM((blocks, 2, GROUP, LANES), BF16)] * 2
    triples = [pltpu.VMEM((blocks, 3, GROUP, LANES), BF16)] * 2
    normed, feature_grad, filter_grad, first, owner = pl.pallas_call(
        block_kernel,
        out_shape=[
            jax.ShapeDtypeStruct((seq_rows, width), BF16),
            jax.ShapeDtypeStruct((3, seq_rows, width), BF16),
            jax.ShapeDtypeStruct((seq_rows, width), BF16),
            jax.ShapeDtypeStruct((blocks,) + row, F32),
            jax.ShapeDtypeStruct((blocks,) + row, F32),
        ],
        in_specs=[VMEM] * 5,
        out_specs=[VMEM] * 5,
        scratch_shapes=exchanged
        + pairs
        + exchanged
        + exchanged
        + triples
        + [pltpu.VMEM((16, width), BF16)] * 3
        + [
            pltpu.VMEM((8, LANES), F32),
            pltpu.VMEM((8, 8, LANES), F32),
            pltpu.VMEM((32,) + row, F32),
            pltpu.VMEM((32,) + row, F32),
            pltpu.VMEM(row, F32),
            pltpu.VMEM((blocks,) + row, F32),
            pltpu.VMEM(row, F32),
            pltpu.VMEM((blocks,) + row, F32),
            pltpu.VMEM((width, LANES), F32),
            pltpu.VMEM((seq_rows + 8, width), F32),
            pltpu.VMEM((seq_rows, width), F32),
            pltpu.VMEM((seq_rows, width), F32),
            pltpu.VMEM(((blocks + 2) * GROUP, LANES), F32),
        ]
        + [pltpu.VMEM(flat, F32)] * 4
        + [pltpu.VMEM(padded, F32)] * 3
        + [pltpu.SemaphoreType.DMA((11, 2))],
        compiler_params=pltpu.CompilerParams(
            collective_id=0, has_side_effects=True, vmem_limit_bytes=48 << 20
        ),
    )(features, short_taps, long_filter, gain[None, :], out_grad)
    first = first.reshape(4, 2, 8, LANES).sum(axis=1).reshape(TAPS + 1, width)
    owner = owner.reshape(blocks, LANES)[:, : 2 * TAPS * GROUP].reshape(blocks, 2, TAPS, GROUP)
    owner = owner.transpose(1, 2, 0, 3).reshape(2, TAPS, width)
    taps_grad = jnp.concatenate([first[None, :TAPS], owner], axis=0)
    return (normed, feature_grad, filter_grad, taps_grad, first[TAPS])


def solution(mesh):
    return jax.shard_map(
        per_device,
        mesh=mesh,
        in_specs=(
            P(None, "ctx", "tp"),
            P(None, None, "tp"),
            P("ctx", "tp"),
            P("tp"),
            P("ctx", "tp"),
        ),
        out_specs=(
            P("ctx", "tp"),
            P(None, "ctx", "tp"),
            P("ctx", "tp"),
            P(None, None, "tp"),
            P("tp"),
        ),
        check_vma=False,
    )
```

time: 1170 us -> 124 us (0.11)
  the two profiles are of different devices: /device:TPU:1 before, /device:TPU:32 now
where the time goes in v2:
time: 124 us
  Pallas kernels  115 us (93%)
  local copies, waits for them, and re-layouts  8.09 us (7%)
    pallas_call x1, Pallas kernels, per_device(): pl.pallas_call(block_kernel, out_shape=[jax.ShapeDtypeStruct((seq_rows, w...  115 us
    unnamed x14, local copies, waits for them, and re-layouts  6.97 us

profile of v2, /device:TPU:32, one launch (start us, length us, event | category | flops | bytes accessed | tf_op | source)
XLA Modules:
  0.0 123.7 jit_solution(16828969683308921280)
XLA Ops:
  0.6 0.0 copy-start
  0.6 1.0 copy-done
  1.6 0.0 copy-start.1
  1.6 0.9 copy-done.1
  2.5 0.0 copy-start.2
  2.5 0.9 copy-done.2
  3.4 0.0 copy-start.3
  3.4 0.8 copy-done.3
  4.2 0.0 copy-start.4
  4.2 0.7 copy-done.4
  4.9 114.9 %shard_map.92 = (bf16[128,512]{1,0:T(8,128)(2,1)S(1)}, bf16[3,128,512]{2,1,0:T(8,128)(2,1)S(1)}, bf16[128,512]{1,0:T(8,128)(2,1)S(1)}, f32[64,1,128]{2,1,0:T(1,128)S(1)}, f32[64,1,128]{2,1,0:T(1,128)S(1)}) custom-call(bf16[3,128,512]{2,1,0:T(8,128)(2,1)S(1)} %copy-done, f32[3,7,512]{2,1,0:T(8,128)S(1)} %copy-done.3, bf16[128,512]{1,0:T(8,128)(2,1)S(1)} %copy-done.1, ...), custom_call_target="tpu_custom_call" | custom-call | tf_op jit(solution)/shard_map/pallas_call | solution.py:446
  119.9 0.6 slice.14
  120.4 0.1 copy.11
  120.5 0.2 copy.12
  120.7 0.3 reshape.29
  121.0 0.6 copy.13
  121.7 0.7 copy.17
  122.3 0.7 copy.18
  123.1 0.7 copy.19
  (4 shorter events, 0.1 us)
Async XLA Ops:
  0.6 1.0 copy-start
  1.6 0.9 copy-start.1
  2.5 0.9 copy-start.2
  3.4 0.8 copy-start.3
  4.2 0.7 copy-start.4

commit v3 on v2

--- a/solution.py
+++ b/solution.py
@@ -15,28 +15,25 @@
 TAPS = 7
 LANES = 128
 GROUP = 8
-VMEM = pl.BlockSpec(memory_space=pltpu.VMEM)
+HBM = pl.BlockSpec(memory_space=pltpu.HBM)
 
 
 def lane_chunks(width):
     return [slice(start, start + LANES) for start in range(0, width, LANES)]
 
 
-def each_partner(me, visit, crossing=True, within=True):
+def each_partner(me, visit, same_half=False):
     row, half, col = me // 16, (me // 8) % 2, me % 8
 
-    def other_half(step, carry):
-        visit(((row + step // 8) % 4) * 16 + (1 - half) * 8 + (col + step % 8) % 8)
+    def one(step, carry):
+        if same_half:
+            visit(((row + 2 + step // 8) % 4) * 16 + half * 8 + (col + step % 8) % 8)
+        else:
+            side = (half + (step // 8) % 2) % 2
+            visit(((row + 2 + step // 16) % 4) * 16 + side * 8 + (col + step % 8) % 8)
         return carry
 
-    def same_half(step, carry):
-        visit(((row + step // 8) % 4) * 16 + half * 8 + (col + step % 8) % 8)
-        return carry
-
-    if crossing:
-        lax.fori_loop(0, 32, other_half, 0)
-    if within:
-        lax.fori_loop(1, 32, same_half, 0)
+    lax.fori_loop(0, 32 if same_half else 64, one, 0)
 
 
 def remote(source, target, sems, device):
@@ -50,25 +47,22 @@
     )
 
 
-def start_exchange(me, source, target, sems):
+def start_exchange(me, across, source, target, sems):
     def visit(partner):
-        remote(source.at[partner], target.at[me], sems, {"ctx": partner}).start()
+        remote(source.at[partner], target.at[me], sems, {"ctx": partner, "tp": across}).start()
 
     each_partner(me, visit)
-    target[pl.ds(me, 1)] = source[pl.ds(me, 1)]
-
-
-def start_gather(me, piece, target, sems):
+
+
+def start_gather(me, across, piece, target, sems):
     def visit(partner):
-        remote(piece, target.at[me], sems, {"ctx": partner}).start()
+        remote(piece, target.at[me], sems, {"ctx": partner, "tp": across}).start()
 
     each_partner(me, visit)
-    target[pl.ds(me, 1)] = piece[...][None]
-
-
-def await_slots(ref, count, sem):
-    slots = ref.at[pl.ds(0, count)]
-    pltpu.make_async_copy(slots, slots, sem).wait()
+
+
+def await_slots(ref, sem):
+    pltpu.make_async_copy(ref, ref, sem).wait()
 
 
 def toeplitz_rows(current, other, first, backward):
@@ -107,7 +101,51 @@
     windows[pl.ds(GROUP, rows), :] = pieces[...].astype(F32).reshape(rows, LANES)
 
 
-def long_products(backward, windows, padded, flat):
+def toeplitz_block(windows, chan, lag, backward):
+    base = pl.multiple_of((lag + 1) * GROUP, GROUP) + chan
+    current = windows[pl.ds(base, 1), :]
+    other = windows[pl.ds(base + (GROUP if backward else -GROUP), 1), :]
+    return [
+        toeplitz_rows(current, other, first, backward).astype(BF16) for first in range(0, LANES, 16)
+    ]
+
+
+def build_toeplitz(windows, toeplitz):
+    blocks = toeplitz.shape[1] // LANES
+
+    def channel(chan, carry):
+        def lags(lag, inner):
+            rows = toeplitz_block(windows, chan, lag, False)
+            for i, part in enumerate(rows):
+                toeplitz[chan, pl.ds(pl.multiple_of(lag * LANES, LANES) + 16 * i, 16), :] = part
+            return inner
+
+        return lax.fori_loop(0, blocks, lags, carry, unroll=16)
+
+    lax.fori_loop(0, GROUP, channel, 0)
+
+
+def causal_products(toeplitz, padded, flat):
+    blocks = padded.shape[1] // 2
+
+    def channel(chan, carry):
+        def two_lags(pair, total):
+            left = [padded[chan, pl.ds(blocks - 2 * pair - i, blocks), :] for i in range(2)]
+            right = toeplitz[chan, pl.ds(pl.multiple_of(pair * 2 * LANES, 2 * LANES), 2 * LANES), :]
+            return total + jnp.dot(
+                jnp.concatenate(left, axis=1).astype(BF16), right, preferred_element_type=F32
+            )
+
+        total = lax.fori_loop(
+            0, blocks // 2, two_lags, jnp.zeros((blocks, LANES), F32), unroll=blocks // 2
+        )
+        flat[pl.ds(chan, blocks, stride=GROUP), :] = total
+        return carry
+
+    lax.fori_loop(0, GROUP, channel, 0)
+
+
+def lagged_products(windows, padded, flat):
     count = len(padded)
     blocks = padded[0].shape[1] // 2
 
@@ -115,14 +153,9 @@
         def two_lags(pair, total):
             left, right = [], []
             for lag in (2 * pair, 2 * pair + 1):
-                base = pl.multiple_of((lag + 1) * GROUP, GROUP) + chan
-                current = windows[pl.ds(base, 1), :]
-                other = windows[pl.ds(base + (GROUP if backward else -GROUP), 1), :]
-                for first in range(0, LANES, 16):
-                    right.append(toeplitz_rows(current, other, first, backward).astype(BF16))
-                start = lag + 1 if backward else blocks - lag
+                right += toeplitz_block(windows, chan, lag, True)
                 left.append(
-                    jnp.concatenate([pad[chan, pl.ds(start, blocks), :] for pad in padded], axis=0)
+                    jnp.concatenate([pad[chan, pl.ds(lag + 1, blocks), :] for pad in padded], axis=0)
                 )
             return total + jnp.dot(
                 jnp.concatenate(left, axis=1).astype(BF16),
@@ -204,16 +237,26 @@
 
 
 def block_kernel(
+    features_hbm,
+    taps_hbm,
+    filter_hbm,
+    gain_hbm,
+    grad_hbm,
+    normed_hbm,
+    feature_grad_hbm,
+    filter_grad_hbm,
+    taps_grad_hbm,
+    gain_grad_hbm,
+    normed_ref,
+    feature_grad_ref,
+    filter_grad_ref,
+    taps_grad_ref,
+    gain_grad_ref,
     features_ref,
     taps_ref,
     filter_ref,
     gain_ref,
     grad_ref,
-    normed_ref,
-    feature_grad_ref,
-    filter_grad_ref,
-    first_sums_ref,
-    owner_sums_ref,
     filt_send,
     filt_recv,
     pair_send,
@@ -236,6 +279,7 @@
     owner_sum,
     owner_all,
     taps_turned,
+    taps_recv,
     pad,
     q_short,
     conv,
@@ -247,11 +291,14 @@
     pad_fwd,
     pad_filt,
     pad_prod,
+    toeplitz,
     sems,
+    load_sems,
+    store_sems,
 ):
     me = lax.axis_index("ctx")
     rank = lax.axis_index("tp")
-    half = (me // 8) % 2
+    across = (rank + 4) % 8
     width = filter_ref.shape[1]
     chunks = list(enumerate(lane_chunks(width)))
     blocks = filt_recv.shape[0]
@@ -263,30 +310,52 @@
     barrier = pltpu.get_barrier_semaphore()
 
     def greet(partner):
-        pl.semaphore_signal(barrier, inc=1, device_id={"ctx": partner}, device_id_type=MESH)
-
-    each_partner(me, greet)
+        pl.semaphore_signal(
+            barrier, inc=1, device_id={"ctx": partner, "tp": across}, device_id_type=MESH
+        )
+
+    for device in (following, preceding):
+        pl.semaphore_signal(barrier, inc=1, device_id=device, device_id_type=MESH)
     for step in range(1, 8):
         pl.semaphore_signal(
             barrier, inc=1, device_id={"tp": (rank + step) % 8}, device_id_type=MESH
         )
+    each_partner(me, greet)
+    loads = [
+        pltpu.make_async_copy(source, target, load_sems.at[i])
+        for i, (source, target) in enumerate(
+            (
+                (filter_hbm, filter_ref),
+                (features_hbm, features_ref),
+                (taps_hbm, taps_ref),
+                (gain_hbm, gain_ref),
+                (grad_hbm, grad_ref),
+            )
+        )
+    ]
+    for load in loads:
+        load.start()
+    for load in loads:
+        load.wait()
 
     for index, lanes in chunks:
         spot = pl.ds(16 * index, 16)
         filt_send[spot] = to_pieces(filter_ref[:, lanes].astype(F32))
         pair_send[spot, 0] = to_pieces(features_ref[1, :, lanes].astype(F32))
         pair_send[spot, 1] = to_pieces(features_ref[2, :, lanes].astype(F32))
-    pl.semaphore_wait(barrier, 70)
-    start_exchange(me, filt_send, filt_recv, sems.at[0])
-    start_exchange(me, pair_send, pair_recv, sems.at[1])
-    last = features_ref.at[0, pl.ds(LANES - 16, 16)]
-    remote(last, before_recv, sems.at[2], following).start()
-
     filler = jnp.zeros((LANES - 3 * TAPS, LANES), F32)
     for index, lanes in chunks:
         stack = jnp.concatenate([taps_ref[i, :, lanes] for i in range(3)] + [filler], axis=0)
         taps_turned[pl.ds(LANES * index, LANES), :] = stack.T
-    own_taps = taps_turned[pl.ds(pl.multiple_of(me * GROUP, GROUP), GROUP), :]
+    pl.semaphore_wait(barrier, 73)
+    start_exchange(me, across, filt_send, filt_recv, sems.at[0])
+    start_exchange(me, across, pair_send, pair_recv, sems.at[1])
+    own_taps = taps_turned.at[pl.ds(pl.multiple_of(me * GROUP, GROUP), GROUP)]
+    taps_copy = remote(own_taps, taps_recv, sems.at[11], {"tp": across})
+    taps_copy.start()
+    last = features_ref.at[0, pl.ds(LANES - 16, 16)]
+    remote(last, before_recv, sems.at[2], following).start()
+
     remote(last, before_recv, sems.at[2], following).wait_recv()
     pad[pl.ds(0, 8), :] = jnp.where(me > 0, before_recv[...].astype(F32)[8:, :], 0.0)
     pad[pl.ds(8, LANES), :] = features_ref[0].astype(F32)
@@ -299,21 +368,24 @@
                 ]
             q_short[pl.ds(top, 64), lanes] = running.astype(BF16).astype(F32)
 
-    await_slots(filt_recv, 63, sems.at[0, 1])
+    await_slots(filt_recv, sems.at[0, 1])
     fill_windows(windows, filt_recv)
+    build_toeplitz(windows, toeplitz)
     flat_a[...] = filt_recv[...].astype(F32).reshape(rows, LANES)
     fill_padded(pad_filt, flat_a, True)
-    await_slots(pair_recv, 63, sems.at[1, 1])
-    k_taps, v_taps = owner_taps(own_taps, 1), owner_taps(own_taps, 2)
+    taps_copy.wait_recv()
+    await_slots(pair_recv, sems.at[1, 1])
+    turned = taps_recv[...]
+    k_taps, v_taps = owner_taps(turned, 1), owner_taps(turned, 2)
     owner_short(pair_recv, 0, k_taps, k_short)
     owner_short(pair_recv, 1, v_taps, v_short)
     flat_b[...] = (k_short[...] * v_short[...]).astype(BF16).astype(F32)
     fill_padded(pad_fwd, flat_b, False)
-    long_products(False, windows, [pad_fwd], [flat_a])
+    causal_products(toeplitz, pad_fwd, flat_a)
     conv_send[...] = flat_a[...].reshape(blocks, GROUP, LANES).astype(BF16)
-    start_exchange(me, conv_send, conv_recv, sems.at[3])
+    start_exchange(me, across, conv_send, conv_recv, sems.at[3])
     fill_padded(pad_prod, flat_b, True)
-    await_slots(conv_recv, 63, sems.at[3, 1])
+    await_slots(conv_recv, sems.at[3, 1])
 
     squares = jnp.zeros((LANES, LANES), F32)
     tilts = jnp.zeros((LANES, LANES), F32)
@@ -329,7 +401,7 @@
     for step in range(1, 8):
         remote(row_send, row_recv.at[rank], sems.at[4], {"tp": (rank + step) % 8}).start()
     row_recv[pl.ds(rank, 1)] = row_send[...][None]
-    await_slots(row_recv, 7, sems.at[4, 1])
+    await_slots(row_recv.at[pl.ds(0, 7)], sems.at[4, 1])
     sums = jnp.sum(row_recv[...], axis=0)
     scale = lax.rsqrt(sums[0:1] / channels + norm_eps)
     bend = scale**3 * sums[1:2] / channels
@@ -347,7 +419,7 @@
     for index, lanes in chunks:
         _, q_value, _, _, _, grad_gated = gate(lanes)
         back_send[pl.ds(16 * index, 16)] = to_pieces(grad_gated * q_value)
-    start_exchange(me, back_send, back_recv, sems.at[5])
+    start_exchange(me, across, back_send, back_recv, sems.at[5])
 
     for index, lanes in chunks:
         value, _, gain, upstream, gated, grad_gated = gate(lanes)
@@ -362,21 +434,28 @@
                 first * pad[pl.ds(8 - lag, LANES), lanes], axis=0, keepdims=True
             )
     remote(after_send, after_recv, sems.at[6], preceding).start()
-    mine = (me // 16) * 8 + me % 8
+    store_normed = pltpu.make_async_copy(normed_ref, normed_hbm, store_sems.at[0])
+    store_normed.start()
 
     def send_part(partner):
         place = (partner // 16) * 8 + partner % 8
-        remote(part_send.at[place], part_recv.at[mine], sems.at[7], {"ctx": partner}).start()
-
-    each_partner(me, send_part, crossing=False)
-    part_recv[pl.ds(mine, 1)] = part_send[pl.ds(mine, 1)]
-    await_slots(part_recv, 31, sems.at[7, 1])
+        remote(
+            part_send.at[place], part_recv.at[me], sems.at[7], {"ctx": partner, "tp": across}
+        ).start()
+
+    each_partner(me, send_part)
+    await_slots(part_recv, sems.at[7, 1])
     part_sum[...] = jnp.sum(part_recv[...], axis=0)
-    start_gather(me, part_sum, first_all, sems.at[8])
-
-    await_slots(back_recv, 63, sems.at[5, 1])
+    mine = (me // 16) * 8 + me % 8
+
+    def send_total(partner):
+        remote(part_sum, first_all.at[mine], sems.at[8], {"ctx": partner, "tp": across}).start()
+
+    each_partner(me, send_total, same_half=True)
+
+    await_slots(back_recv, sems.at[5, 1])
     fill_windows(windows, back_recv)
-    long_products(True, windows, [pad_filt, pad_prod], [flat_a, flat_b])
+    lagged_products(windows, [pad_filt, pad_prod], [flat_a, flat_b])
 
     def place_filter(index, carry):
         step = pl.multiple_of((blocks - 1 - index) * GROUP, GROUP)
@@ -386,7 +465,7 @@
     lax.fori_loop(0, blocks, place_filter, 0, unroll=8)
     k_sums = owner_back(pair_recv, 0, k_taps, flat_a, v_short, out_send, 1)
     v_sums = owner_back(pair_recv, 1, v_taps, flat_a, k_short, out_send, 2)
-    start_exchange(me, out_send, out_recv, sems.at[9])
+    start_exchange(me, across, out_send, out_recv, sems.at[9])
     lane_ids = lax.broadcasted_iota(jnp.int32, (GROUP, LANES), 1)
     chan_ids = lax.broadcasted_iota(jnp.int32, (GROUP, LANES), 0)
     packed = jnp.zeros((GROUP, LANES), F32)
@@ -394,7 +473,7 @@
         total = jnp.sum(value, axis=1, keepdims=True)
         packed = packed + jnp.where(lane_ids == place * GROUP + chan_ids, total, 0.0)
     owner_sum[...] = jnp.sum(packed, axis=0, keepdims=True)
-    start_gather(me, owner_sum, owner_all, sems.at[10])
+    start_gather(me, across, owner_sum, owner_all, sems.at[10])
 
     remote(after_send, after_recv, sems.at[6], preceding).wait_recv()
     pad[pl.ds(0, LANES), :] = conv[...]
@@ -406,31 +485,71 @@
                 total = total + taps_ref[0, lag : lag + 1, lanes] * pad[pl.ds(lag + top, 64), lanes]
             feature_grad_ref[0, pl.ds(top, 64), lanes] = total.astype(BF16)
 
-    await_slots(first_all, 63, sems.at[8, 1])
-    first_sums_ref[...] = first_all[...]
-    await_slots(out_recv, 63, sems.at[9, 1])
+    await_slots(first_all, sems.at[8, 1])
     for index, lanes in chunks:
-        spot = pl.ds(16 * index, 16)
-        filter_grad_ref[:, lanes] = from_pieces(out_recv[spot, 0]).astype(BF16)
-        feature_grad_ref[1, :, lanes] = from_pieces(out_recv[spot, 1]).astype(BF16)
-        feature_grad_ref[2, :, lanes] = from_pieces(out_recv[spot, 2]).astype(BF16)
-    await_slots(owner_all, 63, sems.at[10, 1])
-    owner_sums_ref[...] = owner_all[...]
-
-    for ref, count, number in (
-        (filt_recv, 63, 0),
-        (pair_recv, 63, 1),
-        (conv_recv, 63, 3),
-        (row_recv, 7, 4),
-        (back_recv, 63, 5),
-        (part_recv, 31, 7),
-        (first_all, 63, 8),
-        (out_recv, 63, 9),
-        (owner_all, 63, 10),
+        for lag in range(TAPS):
+            taps_grad_ref[0, lag : lag + 1, lanes] = first_all[lag * len(chunks) + index]
+        gain_grad_ref[:, lanes] = first_all[TAPS * len(chunks) + index]
+    await_slots(owner_all, sems.at[10, 1])
+    lane_ids = lax.broadcasted_iota(jnp.int32, (16, LANES), 1)
+    row_ids = lax.broadcasted_iota(jnp.int32, (16, LANES), 0)
+    for index, lanes in chunks:
+        owned = owner_all[pl.ds(16 * index, 16)].reshape(16, LANES)
+        owned = pltpu.roll(owned, 0, 1, stride=GROUP, stride_axis=0)
+        for place in range(2 * TAPS):
+            turned = pltpu.roll(owned, (LANES - GROUP * place) % LANES, 1) if place else owned
+            value = jnp.where(lane_ids // GROUP == row_ids, turned, 0.0)
+            taps_grad_ref[1 + place // TAPS, pl.ds(place % TAPS, 1), lanes] = jnp.sum(
+                value, axis=0, keepdims=True
+            )
+    stores = [
+        pltpu.make_async_copy(feature_grad_ref.at[0], feature_grad_hbm.at[0], store_sems.at[1]),
+        pltpu.make_async_copy(taps_grad_ref, taps_grad_hbm, store_sems.at[2]),
+        pltpu.make_async_copy(gain_grad_ref, gain_grad_hbm, store_sems.at[3]),
+    ]
+    for store in stores:
+        store.start()
+
+    await_slots(out_recv, sems.at[9, 1])
+    for place, (target, hbm) in enumerate(
+        (
+            (filter_grad_ref, filter_grad_hbm),
+            (feature_grad_ref.at[1], feature_grad_hbm.at[1]),
+            (feature_grad_ref.at[2], feature_grad_hbm.at[2]),
+        )
     ):
-        await_slots(ref, count, sems.at[number, 0])
+        for index, lanes in chunks:
+            target[:, lanes] = from_pieces(out_recv[pl.ds(16 * index, 16), place]).astype(BF16)
+        store = pltpu.make_async_copy(target, hbm, store_sems.at[4 + place])
+        store.start()
+        stores.append(store)
+
+    for ref, number in (
+        (filt_recv, 0),
+        (pair_recv, 1),
+        (conv_recv, 3),
+        (row_recv.at[pl.ds(0, 7)], 4),
+        (back_recv, 5),
+        (part_recv, 7),
+        (first_all, 8),
+        (out_recv, 9),
+        (owner_all, 10),
+    ):
+        await_slots(ref, sems.at[number, 0])
+    taps_copy.wait_send()
+    store_normed.wait()
+    for store in stores:
+        store.wait()
     remote(last, before_recv, sems.at[2], following).wait_send()
     remote(after_send, after_recv, sems.at[6], preceding).wait_send()
+
+
+def hand_on_kernel(*refs):
+    copies = [pltpu.make_async_copy(refs[i], refs[5 + i], refs[10].at[i]) for i in range(5)]
+    for copy in copies:
+        copy.start()
+    for copy in copies:
+        copy.wait()
 
 
 def per_device(features, short_taps, long_filter, gain, out_grad):
@@ -443,18 +562,27 @@
     exchanged = [pltpu.VMEM(pieces, BF16)] * 2
     pairs = [pltpu.VMEM((blocks, 2, GROUP, LANES), BF16)] * 2
     triples = [pltpu.VMEM((blocks, 3, GROUP, LANES), BF16)] * 2
-    normed, feature_grad, filter_grad, first, owner = pl.pallas_call(
+    outs = [
+        jax.ShapeDtypeStruct((seq_rows, width), BF16),
+        jax.ShapeDtypeStruct((3, seq_rows, width), BF16),
+        jax.ShapeDtypeStruct((seq_rows, width), BF16),
+        jax.ShapeDtypeStruct((3, TAPS, width), F32),
+        jax.ShapeDtypeStruct((1, width), F32),
+    ]
+    results = pl.pallas_call(
         block_kernel,
-        out_shape=[
-            jax.ShapeDtypeStruct((seq_rows, width), BF16),
-            jax.ShapeDtypeStruct((3, seq_rows, width), BF16),
-            jax.ShapeDtypeStruct((seq_rows, width), BF16),
-            jax.ShapeDtypeStruct((blocks,) + row, F32),
-            jax.ShapeDtypeStruct((blocks,) + row, F32),
-        ],
-        in_specs=[VMEM] * 5,
-        out_specs=[VMEM] * 5,
-        scratch_shapes=exchanged
+        out_shape=outs,
+        in_specs=[HBM] * 5,
+        out_specs=[HBM] * 5,
+        scratch_shapes=[pltpu.VMEM(out.shape, out.dtype) for out in outs]
+        + [
+            pltpu.VMEM((3, seq_rows, width), BF16),
+            pltpu.VMEM(short_taps.shape, F32),
+            pltpu.VMEM((seq_rows, width), BF16),
+            pltpu.VMEM((1, width), F32),
+            pltpu.VMEM((seq_rows, width), BF16),
+        ]
+        + exchanged
         + pairs
         + exchanged
         + exchanged
@@ -463,13 +591,14 @@
         + [
             pltpu.VMEM((8, LANES), F32),
             pltpu.VMEM((8, 8, LANES), F32),
-            pltpu.VMEM((32,) + row, F32),
-            pltpu.VMEM((32,) + row, F32),
+            pltpu.VMEM((blocks // 2,) + row, F32),
+            pltpu.VMEM((blocks,) + row, F32),
             pltpu.VMEM(row, F32),
-            pltpu.VMEM((blocks,) + row, F32),
+            pltpu.VMEM((blocks // 2,) + row, F32),
             pltpu.VMEM(row, F32),
             pltpu.VMEM((blocks,) + row, F32),
             pltpu.VMEM((width, LANES), F32),
+            pltpu.VMEM((GROUP, LANES), F32),
             pltpu.VMEM((seq_rows + 8, width), F32),
             pltpu.VMEM((seq_rows, width), F32),
             pltpu.VMEM((seq_rows, width), F32),
@@ -477,16 +606,20 @@
         ]
         + [pltpu.VMEM(flat, F32)] * 4
         + [pltpu.VMEM(padded, F32)] * 3
-        + [pltpu.SemaphoreType.DMA((11, 2))],
+        + [pltpu.VMEM((GROUP, blocks * LANES, LANES), BF16)]
+        + [pltpu.SemaphoreType.DMA((12, 2)), pltpu.SemaphoreType.DMA((5,)), pltpu.SemaphoreType.DMA((7,))],
         compiler_params=pltpu.CompilerParams(
-            collective_id=0, has_side_effects=True, vmem_limit_bytes=48 << 20
+            collective_id=0, has_side_effects=True, vmem_limit_bytes=60 << 20
         ),
     )(features, short_taps, long_filter, gain[None, :], out_grad)
-    first = first.reshape(4, 2, 8, LANES).sum(axis=1).reshape(TAPS + 1, width)
-    owner = owner.reshape(blocks, LANES)[:, : 2 * TAPS * GROUP].reshape(blocks, 2, TAPS, GROUP)
-    owner = owner.transpose(1, 2, 0, 3).reshape(2, TAPS, width)
-    taps_grad = jnp.concatenate([first[None, :TAPS], owner], axis=0)
-    return (normed, feature_grad, filter_grad, taps_grad, first[TAPS])
+    normed, feature_grad, filter_grad, taps_grad, gain_grad = pl.pallas_call(
+        hand_on_kernel,
+        out_shape=outs,
+        in_specs=[HBM] * 5,
+        out_specs=[HBM] * 5,
+        scratch_shapes=[pltpu.SemaphoreType.DMA((5,))],
+    )(*results)
+    return (normed, feature_grad, filter_grad, taps_grad, gain_grad[0])
 
 
 def solution(mesh):

time: 124 us -> 141 us (1.14)
  the two profiles are of different devices: /device:TPU:32 before, /device:TPU:1 now
where the time goes in v3:
time: 141 us; the launch traced here: 140 us
  Pallas kernels  140 us (99%)
    pallas_call x1, Pallas kernels, per_device(): pl.pallas_call(block_kernel, out_shape=outs, in_specs=[HBM] * 5, out_spec...  117 us
    pallas_call x1, Pallas kernels, per_device(): pl.pallas_call(hand_on_kernel, out_shape=outs, in_specs=[HBM] * 5, out_sp...  22.6 us

profile of v3, /device:TPU:1, one launch (start us, length us, event | category | flops | bytes accessed | tf_op | source)
XLA Modules:
  0.0 140.4 jit_solution(7554678923934806065)
XLA Ops:
  0.6 117.2 %shard_map.92 = (bf16[128,512]{1,0:T(8,128)(2,1)}, bf16[3,128,512]{2,1,0:T(8,128)(2,1)}, bf16[128,512]{1,0:T(8,128)(2,1)}, f32[3,7,512]{2,1,0:T(8,128)}, f32[1,512]{1,0:T(1,128)}) custom-call(bf16[3,128,512]{2,1,0:T(8,128)(2,1)} %features_hbm.1, f32[3,7,512]{2,1,0:T(8,128)} %taps_hbm.1, bf16[128,512]{1,0:T(8,128)(2,1)} %filter_hbm.1, f32[1,512]{1,0:T(1,128)} %bitcast.2, ...), custom_call_target="tpu_custom_call" | custom-call | tf_op jit(solution)/shard_map/pallas_call | solution.py:572
  117.9 22.6 %shard_map.93 = (bf16[128,512]{1,0:T(8,128)(2,1)}, bf16[3,128,512]{2,1,0:T(8,128)(2,1)}, bf16[128,512]{1,0:T(8,128)(2,1)}, f32[3,7,512]{2,1,0:T(8,128)}, f32[1,512]{1,0:T(1,128)}) custom-call(bf16[128,512]{1,0:T(8,128)(2,1)} %get-tuple-element.15.refs_0_, bf16[3,128,512]{2,1,0:T(8,128)(2,1)} %get-tuple-element.16.refs_1_, ...), custom_call_target="tpu_custom_call" | custom-call | tf_op jit(solution)/shard_map/pallas_call | solution.py:615

commit v4 on v3

--- a/solution.py
+++ b/solution.py
@@ -22,18 +22,22 @@
     return [slice(start, start + LANES) for start in range(0, width, LANES)]
 
 
-def each_partner(me, visit, same_half=False):
+def each_partner(me, visit):
+    def one(step, carry):
+        visit((me + step) % 64)
+        return carry
+
+    lax.fori_loop(0, 64, one, 0)
+
+
+def each_of_half(me, visit):
     row, half, col = me // 16, (me // 8) % 2, me % 8
 
     def one(step, carry):
-        if same_half:
-            visit(((row + 2 + step // 8) % 4) * 16 + half * 8 + (col + step % 8) % 8)
-        else:
-            side = (half + (step // 8) % 2) % 2
-            visit(((row + 2 + step // 16) % 4) * 16 + side * 8 + (col + step % 8) % 8)
+        visit(((row + step // 8) % 4) * 16 + half * 8 + (col + step % 8) % 8)
         return carry
 
-    lax.fori_loop(0, 32 if same_half else 64, one, 0)
+    lax.fori_loop(0, 32, one, 0)
 
 
 def remote(source, target, sems, device):
@@ -265,6 +269,8 @@
     conv_recv,
     back_send,
     back_recv,
+    lag_send,
+    lag_recv,
     out_send,
     out_recv,
     before_recv,
@@ -451,7 +457,7 @@
     def send_total(partner):
         remote(part_sum, first_all.at[mine], sems.at[8], {"ctx": partner, "tp": across}).start()
 
-    each_partner(me, send_total, same_half=True)
+    each_of_half(me, send_total)
 
     await_slots(back_recv, sems.at[5, 1])
     fill_windows(windows, back_recv)
@@ -459,12 +465,13 @@
 
     def place_filter(index, carry):
         step = pl.multiple_of((blocks - 1 - index) * GROUP, GROUP)
-        out_send[index, 0] = flat_b[pl.ds(step, GROUP), :].astype(BF16)
+        lag_send[index] = flat_b[pl.ds(step, GROUP), :].astype(BF16)
         return carry
 
     lax.fori_loop(0, blocks, place_filter, 0, unroll=8)
-    k_sums = owner_back(pair_recv, 0, k_taps, flat_a, v_short, out_send, 1)
-    v_sums = owner_back(pair_recv, 1, v_taps, flat_a, k_short, out_send, 2)
+    start_exchange(me, across, lag_send, lag_recv, sems.at[12])
+    k_sums = owner_back(pair_recv, 0, k_taps, flat_a, v_short, out_send, 0)
+    v_sums = owner_back(pair_recv, 1, v_taps, flat_a, k_short, out_send, 1)
     start_exchange(me, across, out_send, out_recv, sems.at[9])
     lane_ids = lax.broadcasted_iota(jnp.int32, (GROUP, LANES), 1)
     chan_ids = lax.broadcasted_iota(jnp.int32, (GROUP, LANES), 0)
@@ -510,19 +517,23 @@
     for store in stores:
         store.start()
 
-    await_slots(out_recv, sems.at[9, 1])
-    for place, (target, hbm) in enumerate(
-        (
-            (filter_grad_ref, filter_grad_hbm),
-            (feature_grad_ref.at[1], feature_grad_hbm.at[1]),
-            (feature_grad_ref.at[2], feature_grad_hbm.at[2]),
-        )
-    ):
+    def finish(pieces, target, hbm, number):
         for index, lanes in chunks:
-            target[:, lanes] = from_pieces(out_recv[pl.ds(16 * index, 16), place]).astype(BF16)
-        store = pltpu.make_async_copy(target, hbm, store_sems.at[4 + place])
+            target[:, lanes] = from_pieces(pieces(pl.ds(16 * index, 16))).astype(BF16)
+        store = pltpu.make_async_copy(target, hbm, store_sems.at[number])
         store.start()
         stores.append(store)
+
+    await_slots(lag_recv, sems.at[12, 1])
+    finish(lambda spot: lag_recv[spot], filter_grad_ref, filter_grad_hbm, 4)
+    await_slots(out_recv, sems.at[9, 1])
+    for stream in (1, 2):
+        finish(
+            lambda spot, stream=stream: out_recv[spot, stream - 1],
+            feature_grad_ref.at[stream],
+            feature_grad_hbm.at[stream],
+            4 + stream,
+        )
 
     for ref, number in (
         (filt_recv, 0),
@@ -533,6 +544,7 @@
         (part_recv, 7),
         (first_all, 8),
         (out_recv, 9),
+        (lag_recv, 12),
         (owner_all, 10),
     ):
         await_slots(ref, sems.at[number, 0])
@@ -545,11 +557,17 @@
 
 
 def hand_on_kernel(*refs):
-    copies = [pltpu.make_async_copy(refs[i], refs[5 + i], refs[10].at[i]) for i in range(5)]
-    for copy in copies:
-        copy.start()
-    for copy in copies:
-        copy.wait()
+    sources, targets, stages = refs[:5], refs[5:10], refs[10:15]
+    load_sems, store_sems = refs[15:]
+    loads = [pltpu.make_async_copy(sources[i], stages[i], load_sems.at[i]) for i in range(5)]
+    stores = [pltpu.make_async_copy(stages[i], targets[i], store_sems.at[i]) for i in range(5)]
+    for load in loads:
+        load.start()
+    for load, store in zip(loads, stores):
+        load.wait()
+        store.start()
+    for store in stores:
+        store.wait()
 
 
 def per_device(features, short_taps, long_filter, gain, out_grad):
@@ -561,7 +579,6 @@
     row = (1, LANES)
     exchanged = [pltpu.VMEM(pieces, BF16)] * 2
     pairs = [pltpu.VMEM((blocks, 2, GROUP, LANES), BF16)] * 2
-    triples = [pltpu.VMEM((blocks, 3, GROUP, LANES), BF16)] * 2
     outs = [
         jax.ShapeDtypeStruct((seq_rows, width), BF16),
         jax.ShapeDtypeStruct((3, seq_rows, width), BF16),
@@ -586,7 +603,8 @@
         + pairs
         + exchanged
         + exchanged
-        + triples
+        + exchanged
+        + pairs
         + [pltpu.VMEM((16, width), BF16)] * 3
         + [
             pltpu.VMEM((8, LANES), F32),
@@ -607,7 +625,7 @@
         + [pltpu.VMEM(flat, F32)] * 4
         + [pltpu.VMEM(padded, F32)] * 3
         + [pltpu.VMEM((GROUP, blocks * LANES, LANES), BF16)]
-        + [pltpu.SemaphoreType.DMA((12, 2)), pltpu.SemaphoreType.DMA((5,)), pltpu.SemaphoreType.DMA((7,))],
+        + [pltpu.SemaphoreType.DMA((13, 2)), pltpu.SemaphoreType.DMA((5,)), pltpu.SemaphoreType.DMA((7,))],
         compiler_params=pltpu.CompilerParams(
             collective_id=0, has_side_effects=True, vmem_limit_bytes=60 << 20
         ),
@@ -617,7 +635,9 @@
         out_shape=outs,
         in_specs=[HBM] * 5,
         out_specs=[HBM] * 5,
-        scratch_shapes=[pltpu.SemaphoreType.DMA((5,))],
+        scratch_shapes=[pltpu.VMEM(out.shape, out.dtype) for out in outs]
+        + [pltpu.SemaphoreType.DMA((5,))] * 2,
+        compiler_params=pltpu.CompilerParams(vmem_limit_bytes=60 << 20),
     )(*results)
     return (normed, feature_grad, filter_grad, taps_grad, gain_grad[0])
 

time: 141 us -> 116 us (0.82)
  Pallas kernels: 140 us -> 115 us
    pallas_call x1, Pallas kernels: 22.6 us -> 1.95 us  [per_device(): pl.pallas_call(hand_on_kernel, out_shape=outs, in_specs=[HBM] * 5, out_sp...]
    pallas_call x1, Pallas kernels: 117 us -> 113 us  [per_device(): pl.pallas_call(block_kernel, out_shape=outs, in_specs=[HBM] * 5, out_spec...]
where the time goes in v4:
time: 116 us
  Pallas kernels  115 us (99%)
    pallas_call x1, Pallas kernels, per_device(): pl.pallas_call(block_kernel, out_shape=outs, in_specs=[HBM] * 5, out_spec...  113 us

profile of v4, /device:TPU:1, one launch (start us, length us, event | category | flops | bytes accessed | tf_op | source)
XLA Modules:
  0.0 116.1 jit_solution(1625955448624115418)
XLA Ops:
  0.6 113.5 %shard_map.92 = (bf16[128,512]{1,0:T(8,128)(2,1)}, bf16[3,128,512]{2,1,0:T(8,128)(2,1)}, bf16[128,512]{1,0:T(8,128)(2,1)}, f32[3,7,512]{2,1,0:T(8,128)}, f32[1,512]{1,0:T(1,128)}) custom-call(bf16[3,128,512]{2,1,0:T(8,128)(2,1)} %features_hbm.1, f32[3,7,512]{2,1,0:T(8,128)} %taps_hbm.1, bf16[128,512]{1,0:T(8,128)(2,1)} %filter_hbm.1, f32[1,512]{1,0:T(1,128)} %bitcast.2, ...), custom_call_target="tpu_custom_call" | custom-call | tf_op jit(solution)/shard_map/pallas_call | solution.py:589
  114.1 1.9 %shard_map.93 = (bf16[128,512]{1,0:T(8,128)(2,1)}, bf16[3,128,512]{2,1,0:T(8,128)(2,1)}, bf16[128,512]{1,0:T(8,128)(2,1)}, f32[3,7,512]{2,1,0:T(8,128)}, f32[1,512]{1,0:T(1,128)}) custom-call(bf16[128,512]{1,0:T(8,128)(2,1)} %get-tuple-element.15.refs_0_, bf16[3,128,512]{2,1,0:T(8,128)(2,1)} %get-tuple-element.16.refs_1_, ...), custom_call_target="tpu_custom_call" | custom-call | tf_op jit(solution)/shard_map/pallas_call | solution.py:633

commit v5 on v4

--- a/solution.py
+++ b/solution.py
@@ -124,7 +124,7 @@
                 toeplitz[chan, pl.ds(pl.multiple_of(lag * LANES, LANES) + 16 * i, 16), :] = part
             return inner
 
-        return lax.fori_loop(0, blocks, lags, carry, unroll=16)
+        return lax.fori_loop(0, blocks, lags, carry, unroll=blocks)
 
     lax.fori_loop(0, GROUP, channel, 0)
 
@@ -146,7 +146,7 @@
         flat[pl.ds(chan, blocks, stride=GROUP), :] = total
         return carry
 
-    lax.fori_loop(0, GROUP, channel, 0)
+    lax.fori_loop(0, GROUP, channel, 0, unroll=2)
 
 
 def lagged_products(windows, padded, flat):
@@ -174,7 +174,7 @@
             work[pl.ds(chan, blocks, stride=GROUP), :] = total[i * blocks : (i + 1) * blocks]
         return carry
 
-    lax.fori_loop(0, GROUP, channel, 0)
+    lax.fori_loop(0, GROUP, channel, 0, unroll=2)
 
 
 def to_pieces(block):
@@ -192,11 +192,11 @@
     ]
 
 
-def owner_short(raw, which, taps, target):
+def owner_short(raw, taps, target):
     lanes = lax.broadcasted_iota(jnp.int32, (GROUP, LANES), 1)
 
     def block(index, before):
-        now = raw[index, which].astype(F32)
+        now = raw[index].astype(F32)
         total = taps[0] * now
         after = []
         for lag in range(1, TAPS):
@@ -210,7 +210,7 @@
     lax.fori_loop(0, raw.shape[0], block, (zero,) * (TAPS - 1), unroll=8)
 
 
-def owner_back(raw, which, taps, grad_flat, partner_flat, target, slot):
+def owner_back(raw, taps, grad_flat, partner_flat, target):
     lanes = lax.broadcasted_iota(jnp.int32, (GROUP, LANES), 1)
     blocks = raw.shape[0]
 
@@ -220,7 +220,7 @@
         grad = grad_flat[pl.ds(pl.multiple_of(step * GROUP, GROUP), GROUP), :].astype(BF16).astype(F32)
         rows = pl.ds(pl.multiple_of(index * GROUP, GROUP), GROUP)
         grad = (grad * partner_flat[rows, :]).astype(BF16).astype(F32)
-        value = raw[index, which].astype(F32)
+        value = raw[index].astype(F32)
         total = taps[0] * grad
         new_sums = [sums[0] + value * grad]
         new_after = []
@@ -230,7 +230,7 @@
             total = total + taps[lag] * moved
             new_sums.append(sums[lag] + value * moved)
             new_after.append(turned)
-        target[index, slot] = total.astype(BF16)
+        target[index] = total.astype(BF16)
         return tuple(new_after), tuple(new_sums)
 
     zero = jnp.zeros((GROUP, LANES), F32)
@@ -263,16 +263,20 @@
     grad_ref,
     filt_send,
     filt_recv,
-    pair_send,
-    pair_recv,
+    k_send,
+    k_recv,
+    v_send,
+    v_recv,
     conv_send,
     conv_recv,
     back_send,
     back_recv,
     lag_send,
     lag_recv,
-    out_send,
-    out_recv,
+    k_back_send,
+    k_back_recv,
+    v_back_send,
+    v_back_recv,
     before_recv,
     after_send,
     after_recv,
@@ -347,20 +351,21 @@
     for index, lanes in chunks:
         spot = pl.ds(16 * index, 16)
         filt_send[spot] = to_pieces(filter_ref[:, lanes].astype(F32))
-        pair_send[spot, 0] = to_pieces(features_ref[1, :, lanes].astype(F32))
-        pair_send[spot, 1] = to_pieces(features_ref[2, :, lanes].astype(F32))
+        k_send[spot] = to_pieces(features_ref[1, :, lanes].astype(F32))
+        v_send[spot] = to_pieces(features_ref[2, :, lanes].astype(F32))
     filler = jnp.zeros((LANES - 3 * TAPS, LANES), F32)
     for index, lanes in chunks:
         stack = jnp.concatenate([taps_ref[i, :, lanes] for i in range(3)] + [filler], axis=0)
         taps_turned[pl.ds(LANES * index, LANES), :] = stack.T
     pl.semaphore_wait(barrier, 73)
     start_exchange(me, across, filt_send, filt_recv, sems.at[0])
-    start_exchange(me, across, pair_send, pair_recv, sems.at[1])
     own_taps = taps_turned.at[pl.ds(pl.multiple_of(me * GROUP, GROUP), GROUP)]
     taps_copy = remote(own_taps, taps_recv, sems.at[11], {"tp": across})
     taps_copy.start()
     last = features_ref.at[0, pl.ds(LANES - 16, 16)]
     remote(last, before_recv, sems.at[2], following).start()
+    start_exchange(me, across, k_send, k_recv, sems.at[1])
+    start_exchange(me, across, v_send, v_recv, sems.at[13])
 
     remote(last, before_recv, sems.at[2], following).wait_recv()
     pad[pl.ds(0, 8), :] = jnp.where(me > 0, before_recv[...].astype(F32)[8:, :], 0.0)
@@ -380,11 +385,12 @@
     flat_a[...] = filt_recv[...].astype(F32).reshape(rows, LANES)
     fill_padded(pad_filt, flat_a, True)
     taps_copy.wait_recv()
-    await_slots(pair_recv, sems.at[1, 1])
     turned = taps_recv[...]
     k_taps, v_taps = owner_taps(turned, 1), owner_taps(turned, 2)
-    owner_short(pair_recv, 0, k_taps, k_short)
-    owner_short(pair_recv, 1, v_taps, v_short)
+    await_slots(k_recv, sems.at[1, 1])
+    owner_short(k_recv, k_taps, k_short)
+    await_slots(v_recv, sems.at[13, 1])
+    owner_short(v_recv, v_taps, v_short)
     flat_b[...] = (k_short[...] * v_short[...]).astype(BF16).astype(F32)
     fill_padded(pad_fwd, flat_b, False)
     causal_products(toeplitz, pad_fwd, flat_a)
@@ -470,9 +476,10 @@
 
     lax.fori_loop(0, blocks, place_filter, 0, unroll=8)
     start_exchange(me, across, lag_send, lag_recv, sems.at[12])
-    k_sums = owner_back(pair_recv, 0, k_taps, flat_a, v_short, out_send, 0)
-    v_sums = owner_back(pair_recv, 1, v_taps, flat_a, k_short, out_send, 1)
-    start_exchange(me, across, out_send, out_recv, sems.at[9])
+    k_sums = owner_back(k_recv, k_taps, flat_a, v_short, k_back_send)
+    start_exchange(me, across, k_back_send, k_back_recv, sems.at[9])
+    v_sums = owner_back(v_recv, v_taps, flat_a, k_short, v_back_send)
+    start_exchange(me, across, v_back_send, v_back_recv, sems.at[14])
     lane_ids = lax.broadcasted_iota(jnp.int32, (GROUP, LANES), 1)
     chan_ids = lax.broadcasted_iota(jnp.int32, (GROUP, LANES), 0)
     packed = jnp.zeros((GROUP, LANES), F32)
@@ -526,10 +533,10 @@
 
     await_slots(lag_recv, sems.at[12, 1])
     finish(lambda spot: lag_recv[spot], filter_grad_ref, filter_grad_hbm, 4)
-    await_slots(out_recv, sems.at[9, 1])
-    for stream in (1, 2):
+    for stream, (pieces, number) in enumerate(((k_back_recv, 9), (v_back_recv, 14)), 1):
+        await_slots(pieces, sems.at[number, 1])
         finish(
-            lambda spot, stream=stream: out_recv[spot, stream - 1],
+            lambda spot, pieces=pieces: pieces[spot],
             feature_grad_ref.at[stream],
             feature_grad_hbm.at[stream],
             4 + stream,
@@ -537,13 +544,15 @@
 
     for ref, number in (
         (filt_recv, 0),
-        (pair_recv, 1),
+        (k_recv, 1),
+        (v_recv, 13),
         (conv_recv, 3),
         (row_recv.at[pl.ds(0, 7)], 4),
         (back_recv, 5),
         (part_recv, 7),
         (first_all, 8),
-        (out_recv, 9),
+        (k_back_recv, 9),
+        (v_back_recv, 14),
         (lag_recv, 12),
         (owner_all, 10),
     ):
@@ -577,8 +586,6 @@
     flat = (blocks * GROUP, LANES)
     padded = (GROUP, 2 * blocks, LANES)
     row = (1, LANES)
-    exchanged = [pltpu.VMEM(pieces, BF16)] * 2
-    pairs = [pltpu.VMEM((blocks, 2, GROUP, LANES), BF16)] * 2
     outs = [
         jax.ShapeDtypeStruct((seq_rows, width), BF16),
         jax.ShapeDtypeStruct((3, seq_rows, width), BF16),
@@ -599,12 +606,7 @@
             pltpu.VMEM((1, width), F32),
             pltpu.VMEM((seq_rows, width), BF16),
         ]
-        + exchanged
-        + pairs
-        + exchanged
-        + exchanged
-        + exchanged
-        + pairs
+        + [pltpu.VMEM(pieces, BF16)] * 16
         + [pltpu.VMEM((16, width), BF16)] * 3
         + [
             pltpu.VMEM((8, LANES), F32),
@@ -625,7 +627,7 @@
         + [pltpu.VMEM(flat, F32)] * 4
         + [pltpu.VMEM(padded, F32)] * 3
         + [pltpu.VMEM((GROUP, blocks * LANES, LANES), BF16)]
-        + [pltpu.SemaphoreType.DMA((13, 2)), pltpu.SemaphoreType.DMA((5,)), pltpu.SemaphoreType.DMA((7,))],
+        + [pltpu.SemaphoreType.DMA((15, 2)), pltpu.SemaphoreType.DMA((5,)), pltpu.SemaphoreType.DMA((7,))],
         compiler_params=pltpu.CompilerParams(
             collective_id=0, has_side_effects=True, vmem_limit_bytes=60 << 20
         ),

time: 116 us -> 111 us (0.957)
  Pallas kernels: 115 us -> 110 us
    pallas_call x1, Pallas kernels: 113 us -> 109 us  [per_device(): pl.pallas_call(block_kernel, out_shape=outs, in_specs=[HBM] * 5, out_spec...]
where the time goes in v5:
time: 111 us
  Pallas kernels  110 us (99%)
    pallas_call x1, Pallas kernels, per_device(): pl.pallas_call(block_kernel, out_shape=outs, in_specs=[HBM] * 5, out_spec...  109 us

profile of v5, /device:TPU:1, one launch (start us, length us, event | category | flops | bytes accessed | tf_op | source)
XLA Modules:
  0.0 111.1 jit_solution(12426008516533606467)
XLA Ops:
  0.6 108.5 %shard_map.92 = (bf16[128,512]{1,0:T(8,128)(2,1)}, bf16[3,128,512]{2,1,0:T(8,128)(2,1)}, bf16[128,512]{1,0:T(8,128)(2,1)}, f32[3,7,512]{2,1,0:T(8,128)}, f32[1,512]{1,0:T(1,128)}) custom-call(bf16[3,128,512]{2,1,0:T(8,128)(2,1)} %features_hbm.1, f32[3,7,512]{2,1,0:T(8,128)} %taps_hbm.1, bf16[128,512]{1,0:T(8,128)(2,1)} %filter_hbm.1, f32[1,512]{1,0:T(1,128)} %bitcast.2, ...), custom_call_target="tpu_custom_call" | custom-call | tf_op jit(solution)/shard_map/pallas_call | solution.py:596
  109.2 1.9 %shard_map.93 = (bf16[128,512]{1,0:T(8,128)(2,1)}, bf16[3,128,512]{2,1,0:T(8,128)(2,1)}, bf16[128,512]{1,0:T(8,128)(2,1)}, f32[3,7,512]{2,1,0:T(8,128)}, f32[1,512]{1,0:T(1,128)}) custom-call(bf16[128,512]{1,0:T(8,128)(2,1)} %get-tuple-element.15.refs_0_, bf16[3,128,512]{2,1,0:T(8,128)(2,1)} %get-tuple-element.16.refs_1_, ...), custom_call_target="tpu_custom_call" | custom-call | tf_op jit(solution)/shard_map/pallas_call | solution.py:635

commit v6 on v5

--- a/solution.py
+++ b/solution.py
@@ -247,13 +247,14 @@
     gain_hbm,
     grad_hbm,
     normed_hbm,
-    feature_grad_hbm,
-    filter_grad_hbm,
+    q_grad_hbm,
     taps_grad_hbm,
     gain_grad_hbm,
+    lag_recv,
+    k_back_recv,
+    v_back_recv,
     normed_ref,
-    feature_grad_ref,
-    filter_grad_ref,
+    q_grad_ref,
     taps_grad_ref,
     gain_grad_ref,
     features_ref,
@@ -272,11 +273,8 @@
     back_send,
     back_recv,
     lag_send,
-    lag_recv,
     k_back_send,
-    k_back_recv,
     v_back_send,
-    v_back_recv,
     before_recv,
     after_send,
     after_recv,
@@ -407,7 +405,6 @@
         gated = q_short[:, lanes] * value
         squares = squares + gated * gated
         tilts = tilts + gain_ref[:, lanes] * grad_ref[:, lanes].astype(F32) * gated
-    row_send[...] = jnp.zeros(row_send.shape, F32)
     row_send[pl.ds(0, 1), :] = jnp.sum(squares.T, axis=0, keepdims=True)
     row_send[pl.ds(1, 1), :] = jnp.sum(tilts.T, axis=0, keepdims=True)
     for step in range(1, 8):
@@ -456,14 +453,6 @@
         ).start()
 
     each_partner(me, send_part)
-    await_slots(part_recv, sems.at[7, 1])
-    part_sum[...] = jnp.sum(part_recv[...], axis=0)
-    mine = (me // 16) * 8 + me % 8
-
-    def send_total(partner):
-        remote(part_sum, first_all.at[mine], sems.at[8], {"ctx": partner, "tp": across}).start()
-
-    each_of_half(me, send_total)
 
     await_slots(back_recv, sems.at[5, 1])
     fill_windows(windows, back_recv)
@@ -489,6 +478,15 @@
     owner_sum[...] = jnp.sum(packed, axis=0, keepdims=True)
     start_gather(me, across, owner_sum, owner_all, sems.at[10])
 
+    await_slots(part_recv, sems.at[7, 1])
+    part_sum[...] = jnp.sum(part_recv[...], axis=0)
+    mine = (me // 16) * 8 + me % 8
+
+    def send_total(partner):
+        remote(part_sum, first_all.at[mine], sems.at[8], {"ctx": partner, "tp": across}).start()
+
+    each_of_half(me, send_total)
+
     remote(after_send, after_recv, sems.at[6], preceding).wait_recv()
     pad[pl.ds(0, LANES), :] = conv[...]
     pad[pl.ds(LANES, 8), :] = jnp.where(me < 63, after_recv[...].astype(F32)[:8, :], 0.0)
@@ -497,7 +495,7 @@
             total = jnp.zeros((64, LANES), F32)
             for lag in range(TAPS):
                 total = total + taps_ref[0, lag : lag + 1, lanes] * pad[pl.ds(lag + top, 64), lanes]
-            feature_grad_ref[0, pl.ds(top, 64), lanes] = total.astype(BF16)
+            q_grad_ref[pl.ds(top, 64), lanes] = total.astype(BF16)
 
     await_slots(first_all, sems.at[8, 1])
     for index, lanes in chunks:
@@ -517,31 +515,15 @@
                 value, axis=0, keepdims=True
             )
     stores = [
-        pltpu.make_async_copy(feature_grad_ref.at[0], feature_grad_hbm.at[0], store_sems.at[1]),
+        pltpu.make_async_copy(q_grad_ref, q_grad_hbm, store_sems.at[1]),
         pltpu.make_async_copy(taps_grad_ref, taps_grad_hbm, store_sems.at[2]),
         pltpu.make_async_copy(gain_grad_ref, gain_grad_hbm, store_sems.at[3]),
     ]
     for store in stores:
         store.start()
 
-    def finish(pieces, target, hbm, number):
-        for index, lanes in chunks:
-            target[:, lanes] = from_pieces(pieces(pl.ds(16 * index, 16))).astype(BF16)
-        store = pltpu.make_async_copy(target, hbm, store_sems.at[number])
-        store.start()
-        stores.append(store)
-
-    await_slots(lag_recv, sems.at[12, 1])
-    finish(lambda spot: lag_recv[spot], filter_grad_ref, filter_grad_hbm, 4)
-    for stream, (pieces, number) in enumerate(((k_back_recv, 9), (v_back_recv, 14)), 1):
-        await_slots(pieces, sems.at[number, 1])
-        finish(
-            lambda spot, pieces=pieces: pieces[spot],
-            feature_grad_ref.at[stream],
-            feature_grad_hbm.at[stream],
-            4 + stream,
-        )
-
+    for ref, number in ((lag_recv, 12), (k_back_recv, 9), (v_back_recv, 14)):
+        await_slots(ref, sems.at[number, 1])
     for ref, number in (
         (filt_recv, 0),
         (k_recv, 1),
@@ -565,18 +547,35 @@
     remote(after_send, after_recv, sems.at[6], preceding).wait_send()
 
 
-def hand_on_kernel(*refs):
-    sources, targets, stages = refs[:5], refs[5:10], refs[10:15]
-    load_sems, store_sems = refs[15:]
-    loads = [pltpu.make_async_copy(sources[i], stages[i], load_sems.at[i]) for i in range(5)]
-    stores = [pltpu.make_async_copy(stages[i], targets[i], store_sems.at[i]) for i in range(5)]
+def closing_kernel(*refs):
+    sources, targets, stages = refs[:7], refs[7:12], refs[12:19]
+    filter_stage, stream_stage, load_sems, store_sems = refs[19:]
+    normed, feature_grad, filter_grad, taps_grad, gain_grad = targets
+    loads = [pltpu.make_async_copy(sources[i], stages[i], load_sems.at[i]) for i in range(7)]
     for load in loads:
         load.start()
-    for load, store in zip(loads, stores):
-        load.wait()
-        store.start()
-    for store in stores:
-        store.wait()
+    stores = []
+
+    def store(source, target):
+        copy = pltpu.make_async_copy(source, target, store_sems.at[len(stores)])
+        copy.start()
+        stores.append(copy)
+
+    for i, target in enumerate((normed, feature_grad.at[0], taps_grad, gain_grad)):
+        loads[i].wait()
+        store(stages[i], target)
+    turned = (
+        (filter_stage, filter_grad),
+        (stream_stage.at[0], feature_grad.at[1]),
+        (stream_stage.at[1], feature_grad.at[2]),
+    )
+    for i, (stage, target) in enumerate(turned, 4):
+        loads[i].wait()
+        for index, lanes in enumerate(lane_chunks(stage.shape[1])):
+            stage[:, lanes] = from_pieces(stages[i][pl.ds(16 * index, 16)]).astype(BF16)
+        store(stage, target)
+    for copy in stores:
+        copy.wait()
 
 
 def per_device(features, short_taps, long_filter, gain, out_grad):
@@ -586,19 +585,17 @@
     flat = (blocks * GROUP, LANES)
     padded = (GROUP, 2 * blocks, LANES)
     row = (1, LANES)
-    outs = [
-        jax.ShapeDtypeStruct((seq_rows, width), BF16),
-        jax.ShapeDtypeStruct((3, seq_rows, width), BF16),
-        jax.ShapeDtypeStruct((seq_rows, width), BF16),
-        jax.ShapeDtypeStruct((3, TAPS, width), F32),
-        jax.ShapeDtypeStruct((1, width), F32),
-    ]
+    plane = jax.ShapeDtypeStruct((seq_rows, width), BF16)
+    taps = jax.ShapeDtypeStruct((3, TAPS, width), F32)
+    gains = jax.ShapeDtypeStruct((1, width), F32)
+    arrivals = [jax.ShapeDtypeStruct(pieces, BF16)] * 3
+    outs = [plane, plane, taps, gains] + arrivals
     results = pl.pallas_call(
         block_kernel,
         out_shape=outs,
         in_specs=[HBM] * 5,
-        out_specs=[HBM] * 5,
-        scratch_shapes=[pltpu.VMEM(out.shape, out.dtype) for out in outs]
+        out_specs=[HBM] * 7,
+        scratch_shapes=[pltpu.VMEM(out.shape, out.dtype) for out in outs[:4]]
         + [
             pltpu.VMEM((3, seq_rows, width), BF16),
             pltpu.VMEM(short_taps.shape, F32),
@@ -606,11 +603,11 @@
             pltpu.VMEM((1, width), F32),
             pltpu.VMEM((seq_rows, width), BF16),
         ]
-        + [pltpu.VMEM(pieces, BF16)] * 16
+        + [pltpu.VMEM(pieces, BF16)] * 13
         + [pltpu.VMEM((16, width), BF16)] * 3
         + [
-            pltpu.VMEM((8, LANES), F32),
-            pltpu.VMEM((8, 8, LANES), F32),
+            pltpu.VMEM((2, LANES), F32),
+            pltpu.VMEM((8, 2, LANES), F32),
             pltpu.VMEM((blocks // 2,) + row, F32),
             pltpu.VMEM((blocks,) + row, F32),
             pltpu.VMEM(row, F32),
@@ -627,18 +624,19 @@
         + [pltpu.VMEM(flat, F32)] * 4
         + [pltpu.VMEM(padded, F32)] * 3
         + [pltpu.VMEM((GROUP, blocks * LANES, LANES), BF16)]
-        + [pltpu.SemaphoreType.DMA((15, 2)), pltpu.SemaphoreType.DMA((5,)), pltpu.SemaphoreType.DMA((7,))],
+        + [pltpu.SemaphoreType.DMA((15, 2)), pltpu.SemaphoreType.DMA((5,)), pltpu.SemaphoreType.DMA((4,))],
         compiler_params=pltpu.CompilerParams(
             collective_id=0, has_side_effects=True, vmem_limit_bytes=60 << 20
         ),
     )(features, short_taps, long_filter, gain[None, :], out_grad)
     normed, feature_grad, filter_grad, taps_grad, gain_grad = pl.pallas_call(
-        hand_on_kernel,
-        out_shape=outs,
-        in_specs=[HBM] * 5,
+        closing_kernel,
+        out_shape=[plane, jax.ShapeDtypeStruct(features.shape, BF16), plane, taps, gains],
+        in_specs=[HBM] * 7,
         out_specs=[HBM] * 5,
         scratch_shapes=[pltpu.VMEM(out.shape, out.dtype) for out in outs]
-        + [pltpu.SemaphoreType.DMA((5,))] * 2,
+        + [pltpu.VMEM((seq_rows, width), BF16), pltpu.VMEM((2, seq_rows, width), BF16)]
+        + [pltpu.SemaphoreType.DMA((7,))] * 2,
         compiler_params=pltpu.CompilerParams(vmem_limit_bytes=60 << 20),
     )(*results)
     return (normed, feature_grad, filter_grad, taps_grad, gain_grad[0])

time: 111 us -> 110 us (level)
  no operation moved by 1% of the time
where the time goes in v6:
time: 110 us
  Pallas kernels  110 us (100%)
    pallas_call x1, Pallas kernels, per_device(): pl.pallas_call(block_kernel, out_shape=outs, in_specs=[HBM] * 5, out_spec...  108 us

profile of v6, /device:TPU:1, one launch (start us, length us, event | category | flops | bytes accessed | tf_op | source)
XLA Modules:
  0.0 110.3 jit_solution(7765481569928807805)
XLA Ops:
  0.6 107.5 %shard_map.92 = (bf16[128,512]{1,0:T(8,128)(2,1)}, bf16[128,512]{1,0:T(8,128)(2,1)}, f32[3,7,512]{2,1,0:T(8,128)}, f32[1,512]{1,0:T(1,128)}, bf16[64,8,128]{2,1,...) custom-call(bf16[3,128,512]{2,1,0:T(8,128)(2,1)} %features_hbm.1, f32[3,7,512]{2,1,0:T(8,128)} %taps_hbm.1, ...), custom_call_target="tpu_custom_call" | custom-call | tf_op jit(solution)/shard_map/pallas_call | solution.py:593
  108.2 2.2 %shard_map.93 = (bf16[128,512]{1,0:T(8,128)(2,1)}, bf16[3,128,512]{2,1,0:T(8,128)(2,1)}, bf16[128,512]{1,0:T(8,128)(2,1)}, f32[3,7,512]{2,1,0:T(8,128)}, f32[1,512]{1,0:T(1,128)}) custom-call(bf16[128,512]{1,0:T(8,128)(2,1)} %get-tuple-element.17.refs_0_, bf16[128,512]{1,0:T(8,128)(2,1)} %get-tuple-element.18.refs_1_, ...), custom_call_target="tpu_custom_call" | custom-call | tf_op jit(solution)/shard_map/pallas_call | solution.py:632

commit v7 on v6

--- a/solution.py
+++ b/solution.py
@@ -146,7 +146,7 @@
         flat[pl.ds(chan, blocks, stride=GROUP), :] = total
         return carry
 
-    lax.fori_loop(0, GROUP, channel, 0, unroll=2)
+    lax.fori_loop(0, GROUP, channel, 0, unroll=4)
 
 
 def lagged_products(windows, padded, flat):
@@ -174,7 +174,7 @@
             work[pl.ds(chan, blocks, stride=GROUP), :] = total[i * blocks : (i + 1) * blocks]
         return carry
 
-    lax.fori_loop(0, GROUP, channel, 0, unroll=2)
+    lax.fori_loop(0, GROUP, channel, 0, unroll=4)
 
 
 def to_pieces(block):
@@ -207,7 +207,7 @@
         return tuple(after)
 
     zero = jnp.zeros((GROUP, LANES), F32)
-    lax.fori_loop(0, raw.shape[0], block, (zero,) * (TAPS - 1), unroll=8)
+    lax.fori_loop(0, raw.shape[0], block, (zero,) * (TAPS - 1), unroll=32)
 
 
 def owner_back(raw, taps, grad_flat, partner_flat, target):
@@ -235,7 +235,7 @@
 
     zero = jnp.zeros((GROUP, LANES), F32)
     _, sums = lax.fori_loop(
-        0, blocks, block, ((zero,) * (TAPS - 1), (zero,) * TAPS), unroll=8
+        0, blocks, block, ((zero,) * (TAPS - 1), (zero,) * TAPS), unroll=16
     )
     return sums
 

time: 110 us -> 109 us (level)
  no operation moved by 1% of the time
where the time goes in v7:
time: 109 us
  Pallas kernels  109 us (100%)
    pallas_call x1, Pallas kernels, per_device(): pl.pallas_call(block_kernel, out_shape=outs, in_specs=[HBM] * 5, out_spec...  107 us

profile of v7, /device:TPU:1, one launch (start us, length us, event | category | flops | bytes accessed | tf_op | source)
XLA Modules:
  0.0 109.3 jit_solution(11199283529564614580)
XLA Ops:
  0.6 106.5 %shard_map.92 = (bf16[128,512]{1,0:T(8,128)(2,1)}, bf16[128,512]{1,0:T(8,128)(2,1)}, f32[3,7,512]{2,1,0:T(8,128)}, f32[1,512]{1,0:T(1,128)}, bf16[64,8,128]{2,1,...) custom-call(bf16[3,128,512]{2,1,0:T(8,128)(2,1)} %features_hbm.1, f32[3,7,512]{2,1,0:T(8,128)} %taps_hbm.1, ...), custom_call_target="tpu_custom_call" | custom-call | tf_op jit(solution)/shard_map/pallas_call | solution.py:593
  107.1 2.2 %shard_map.93 = (bf16[128,512]{1,0:T(8,128)(2,1)}, bf16[3,128,512]{2,1,0:T(8,128)(2,1)}, bf16[128,512]{1,0:T(8,128)(2,1)}, f32[3,7,512]{2,1,0:T(8,128)}, f32[1,512]{1,0:T(1,128)}) custom-call(bf16[128,512]{1,0:T(8,128)(2,1)} %get-tuple-element.17.refs_0_, bf16[128,512]{1,0:T(8,128)(2,1)} %get-tuple-element.18.refs_1_, ...), custom_call_target="tpu_custom_call" | custom-call | tf_op jit(solution)/shard_map/pallas_call | solution.py:632

commit v8 on v7

--- a/solution.py
+++ b/solution.py
@@ -27,7 +27,7 @@
         visit((me + step) % 64)
         return carry
 
-    lax.fori_loop(0, 64, one, 0)
+    lax.fori_loop(0, 64, one, 0, unroll=4)
 
 
 def each_of_half(me, visit):

time: 109 us -> 109 us (level)
  no operation moved by 1% of the time
where the time goes in v8:
time: 109 us
  Pallas kernels  108 us (99%)
    pallas_call x1, Pallas kernels, per_device(): pl.pallas_call(block_kernel, out_shape=outs, in_specs=[HBM] * 5, out_spec...  106 us

profile of v8, /device:TPU:1, one launch (start us, length us, event | category | flops | bytes accessed | tf_op | source)
XLA Modules:
  0.0 108.9 jit_solution(876202204359178501)
XLA Ops:
  0.6 106.1 %shard_map.92 = (bf16[128,512]{1,0:T(8,128)(2,1)}, bf16[128,512]{1,0:T(8,128)(2,1)}, f32[3,7,512]{2,1,0:T(8,128)}, f32[1,512]{1,0:T(1,128)}, bf16[64,8,128]{2,1,...) custom-call(bf16[3,128,512]{2,1,0:T(8,128)(2,1)} %features_hbm.1, f32[3,7,512]{2,1,0:T(8,128)} %taps_hbm.1, ...), custom_call_target="tpu_custom_call" | custom-call | tf_op jit(solution)/shard_map/pallas_call | solution.py:593
  106.7 2.2 %shard_map.93 = (bf16[128,512]{1,0:T(8,128)(2,1)}, bf16[3,128,512]{2,1,0:T(8,128)(2,1)}, bf16[128,512]{1,0:T(8,128)(2,1)}, f32[3,7,512]{2,1,0:T(8,128)}, f32[1,512]{1,0:T(1,128)}) custom-call(bf16[128,512]{1,0:T(8,128)(2,1)} %get-tuple-element.17.refs_0_, bf16[128,512]{1,0:T(8,128)(2,1)} %get-tuple-element.18.refs_1_, ...), custom_call_target="tpu_custom_call" | custom-call | tf_op jit(solution)/shard_map/pallas_call | solution.py:632
